TPU v7x, 32 devices: a whole 2x2x4 slice. The times are simulated.
32 devices in a mesh: row: 8 (over y, x, core), col: 4 (over z).
Axes of the slice: x: 2, y: 2, z: 4, core: 2. Of those that a mesh axis runs over, the one named last changes fastest.
Arguments:
- kernel: bfloat16 [16, 8, 16, 4, 8192], P(None, 'row', None, 'col'), as said below
Outputs:
- factor: float32 [16, 8, 16, 4, 8192], P(None, 'row', None, 'col')
Inputs may be any that keep to these rules, and one draw needn't show every extreme that they name: kernel holds a symmetric positive definite matrix.
All inputs are finite; a program needn't handle non-finite values.
Results may differ from a plain program's by a relative error of at most 0.0046.
Values may be sent and summed in bfloat16 or wider, within the bound.
No kernel may reach another device: no remote copies, remote signals or barrier semaphores. Data moves between devices by JAX's collectives and lax.ppermute only.
A program may use at most 64 MiB of HBM per device.

v0:
```python
import functools

import jax
import jax.numpy as jnp
from jax import lax
from jax.experimental import pallas as pl
from jax.experimental.pallas import tpu as pltpu
from jax.sharding import PartitionSpec as P

P_SIZE = 512
NT = 16
STEP = 16
BLOCK = 128
EXACT = lax.Precision.HIGHEST


def exact_dot(left_side, right_side, contract=((1,), (0,))):
    return lax.dot_general(
        left_side,
        right_side,
        (contract, ((), ())),
        preferred_element_type=jnp.float32,
        precision=EXACT,
    )


def fast_dot(left_side, right_side, contract=((1,), (0,))):
    return lax.dot_general(
        left_side, right_side, (contract, ((), ())), preferred_element_type=jnp.float32
    )


def factor_block(work, done):
    row_id = lax.broadcasted_iota(jnp.int32, (STEP, BLOCK), 0)
    for start in range(0, BLOCK, STEP):
        here = slice(start, start + STEP)
        halves = [work[here, 0:BLOCK], work[here, BLOCK : 2 * BLOCK]]
        columns = [
            jnp.broadcast_to(halves[0][:, start + j : start + j + 1], (STEP, BLOCK))
            for j in range(STEP)
        ]
        raw = work[start + STEP :, here] if start + STEP < BLOCK else None
        kept = [jnp.zeros((STEP, BLOCK), jnp.float32)] * 2
        pivots = jnp.ones((STEP, BLOCK), jnp.float32)
        for k in range(STEP):
            pivot = jnp.broadcast_to(columns[k][k : k + 1, :], (STEP, BLOCK))
            factors = jnp.where(row_id == k, 0.0, columns[k] * (1.0 / pivot))
            for j in range(k + 1, STEP):
                top = jnp.broadcast_to(columns[j][k : k + 1, :], (STEP, BLOCK))
                columns[j] = columns[j] - factors * top
            pivots = jnp.where(row_id == k, pivot, pivots)
            for h in range(2):
                top = jnp.broadcast_to(halves[h][k : k + 1, :], (STEP, BLOCK))
                kept[h] = jnp.where(row_id == k, top, kept[h])
                halves[h] = halves[h] - factors * top
        scale = lax.rsqrt(pivots)
        inverse = 1.0 / pivots
        for h in range(2):
            done[here, h * BLOCK : (h + 1) * BLOCK] = kept[h] * scale
        if raw is not None:
            solved = jnp.concatenate([halves[0] * inverse, halves[1] * inverse], axis=1)
            work[start + STEP :, :] = work[start + STEP :, :] - exact_dot(raw, solved)


def factor_kernel(given, factor, inverse, rest, work, done):
    rest[...] = given[...]
    factor_rest(rest, factor, inverse, work, done)


def factor_rest(rest, factor, inverse, work, done):
    order = rest.shape[0]
    inverse[...] = jnp.zeros_like(inverse)
    factor[...] = jnp.zeros_like(factor)
    row_id = lax.broadcasted_iota(jnp.int32, (BLOCK, BLOCK), 0)
    column_id = lax.broadcasted_iota(jnp.int32, (BLOCK, BLOCK), 1)
    for start in range(0, order, BLOCK):
        here = slice(start, start + BLOCK)
        work[:, 0:BLOCK] = rest[here, here]
        work[:, BLOCK:] = (row_id == column_id).astype(jnp.float32)
        factor_block(work, done)
        factor[here, here] = jnp.where(column_id >= row_id, done[:, 0:BLOCK], 0.0).T
        block_inverse = done[:, BLOCK:]
        if start:
            inverse[here, 0:start] = exact_dot(block_inverse, inverse[here, 0:start])
        inverse[here, here] = block_inverse
        if start + BLOCK < order:
            after = slice(start + BLOCK, order)
            upper = exact_dot(block_inverse, rest[here, after])
            lower = upper.T
            factor[after, here] = lower
            rest[after, after] = rest[after, after] - exact_dot(lower, upper)
            so_far = slice(0, start + BLOCK)
            inverse[after, so_far] = inverse[after, so_far] - exact_dot(
                lower, inverse[here, so_far]
            )


def factor_scratch():
    return [
        pltpu.VMEM((P_SIZE, P_SIZE), jnp.float32),
        pltpu.VMEM((BLOCK, 2 * BLOCK), jnp.float32),
        pltpu.VMEM((BLOCK, 2 * BLOCK), jnp.float32),
    ]


def factor_corner(corner):
    order = corner.shape[0]
    square = jax.ShapeDtypeStruct((order, order), jnp.float32)
    return pl.pallas_call(
        factor_kernel,
        out_shape=[square, square],
        scratch_shapes=factor_scratch(),
        compiler_params=pltpu.CompilerParams(vmem_limit_bytes=32 * 2**20),
    )(corner)


def spread(value, axis, offsets):
    count = lax.axis_size(axis)
    parts = [value]
    for offset in offsets[1:]:
        parts.append(lax.ppermute(value, axis, [(i, i ^ offset) for i in range(count)]))
    return jnp.stack(parts)


def gather_corner(mine):
    row_count = lax.axis_size("row")
    col_count = lax.axis_size("col")
    row_index = lax.axis_index("row")
    column_index = lax.axis_index("col")
    over_cols = spread(mine, "col", list(range(col_count)))
    over_chips = spread(over_cols, "row", list(range(0, row_count, 2)))
    slots = spread(over_chips, "row", [0, 1])
    slots = slots.transpose(1, 0, 2, 3, 4, 5).reshape(row_count, col_count, *mine.shape)
    slots = jnp.take(slots, jnp.arange(row_count) ^ row_index, axis=0, mode="clip")
    slots = jnp.take(slots, jnp.arange(col_count) ^ column_index, axis=1, mode="clip")
    return slots.transpose(2, 0, 3, 1, 4).reshape(3, P_SIZE, P_SIZE)


def per_device_general(kernel):
    row_count = lax.axis_size("row")
    col_count = lax.axis_size("col")
    tile_rows = P_SIZE // row_count
    tile_cols = P_SIZE // col_count
    row_index = lax.axis_index("row")
    column_index = lax.axis_index("col")
    tiles = kernel.reshape(NT, NT, tile_rows, tile_cols)
    corner = gather_corner(jnp.stack([tiles[0, 0], tiles[1, 0], tiles[1, 1]]))
    own_rows = tiles[:, 0:2].transpose(0, 2, 1, 3).reshape(NT * tile_rows, 2 * tile_cols)
    own_rows = lax.all_gather(own_rows, "col", axis=0, tiled=False)
    own_rows = own_rows.reshape(col_count, NT * tile_rows, 2, tile_cols).transpose(1, 2, 0, 3)
    own_rows = own_rows.reshape(NT * tile_rows, 2, P_SIZE)
    own_cols = tiles[0:2].transpose(0, 2, 1, 3).reshape(2 * tile_rows, NT * tile_cols)
    own_cols = lax.all_gather(own_cols, "row", axis=0, tiled=False)
    own_cols = own_cols.reshape(row_count, 2, tile_rows, NT * tile_cols).transpose(1, 0, 2, 3)
    own_cols = own_cols.reshape(2, P_SIZE, NT * tile_cols)

    first_corner, cross_corner, second_corner = (corner[i].astype(jnp.float32) for i in range(3))
    first_factor, first_inverse = factor_corner(0.5 * (first_corner + first_corner.T))
    cross = exact_dot(cross_corner, first_inverse, ((1,), (1,))).astype(jnp.bfloat16)
    updated_corner = second_corner - fast_dot(cross, cross, ((1,), (1,)))
    second_factor, second_inverse = factor_corner(0.5 * (updated_corner + updated_corner.T))

    first_rows = exact_dot(
        own_rows[tile_rows:, 0].astype(jnp.float32), first_inverse, ((1,), (1,))
    )
    first_cols = exact_dot(first_inverse, own_cols[0, :, tile_cols:].astype(jnp.float32))
    first_rows_rounded = first_rows.astype(jnp.bfloat16)
    first_cols_rounded = first_cols.astype(jnp.bfloat16)
    second_rows = own_rows[2 * tile_rows :, 1].astype(jnp.float32) - fast_dot(
        first_rows_rounded[tile_rows:], cross, ((1,), (1,))
    )
    second_cols = own_cols[1, :, 2 * tile_cols :].astype(jnp.float32) - fast_dot(
        cross, first_cols_rounded[:, tile_cols:]
    )
    second_rows = exact_dot(second_rows, second_inverse, ((1,), (1,)))
    second_cols = exact_dot(second_inverse, second_cols)
    left_side = jnp.concatenate(
        [first_rows_rounded[tile_rows:], second_rows.astype(jnp.bfloat16)], axis=1
    )
    right_side = jnp.concatenate(
        [first_cols_rounded[:, tile_cols:], second_cols.astype(jnp.bfloat16)], axis=0
    )
    inner = NT - 2
    product = fast_dot(left_side, right_side).reshape(inner, tile_rows, inner, tile_cols)
    trailing = tiles[2:, 2:].astype(jnp.float32) - product.transpose(0, 2, 1, 3)
    own = (row_index * tile_rows, column_index * tile_cols)
    first_own = lax.dynamic_slice_in_dim(first_rows, own[1], tile_cols, 1)
    second_own = lax.dynamic_slice_in_dim(second_rows, own[1], tile_cols, 1)
    first_tile = lax.dynamic_slice(first_factor, own, (tile_rows, tile_cols))
    second_tile = lax.dynamic_slice(second_factor, own, (tile_rows, tile_cols))
    result = jnp.zeros(tiles.shape, jnp.float32)
    result = result.at[2:, 2:].set(trailing)
    result = result.at[0, 0].set(first_tile)
    result = result.at[1:, 0].set(first_own.reshape(NT - 1, tile_rows, tile_cols))
    result = result.at[1, 1].set(second_tile)
    result = result.at[2:, 1].set(second_own.reshape(NT - 2, tile_rows, tile_cols))
    return result.reshape(kernel.shape)


def whole(shape):
    return pl.BlockSpec(shape, lambda *_: (0,) * len(shape))


def natural_tile(tiles, spread_rows, tile_rows):
    for r in range(tile_rows):
        spread_rows[r * NT : (r + 1) * NT, :] = tiles[:, r * BLOCK : (r + 1) * BLOCK].astype(
            jnp.float32
        )


def top_kernel(tiles, corner, top, spread_rows):
    tile_rows = corner.shape[1]
    for t in range(2):
        natural_tile(tiles[t], spread_rows, tile_rows)
        for s in range(NT):
            tile = spread_rows[pl.ds(s, tile_rows, stride=NT), :].astype(jnp.bfloat16)
            top[t * tile_rows : (t + 1) * tile_rows, s * BLOCK : (s + 1) * BLOCK] = tile
            if s <= t:
                corner[t + s] = tile


def natural_kernel(tiles, natural, left, spread_rows):
    tile_rows = natural.shape[0]
    natural_tile(tiles[0], spread_rows, tile_rows)
    for s in range(NT):
        tile = spread_rows[pl.ds(s, tile_rows, stride=NT), :].astype(jnp.bfloat16)
        natural[:, s * BLOCK : (s + 1) * BLOCK] = tile
        if s < 2:
            left[:, s * BLOCK : (s + 1) * BLOCK] = tile


def take_top(tiles, tile_rows):
    return pl.pallas_call(
        top_kernel,
        grid=(1,),
        in_specs=[pl.BlockSpec((2, NT, tile_rows * BLOCK), lambda i: (0, 0, 0))],
        out_specs=[whole((3, tile_rows, BLOCK)), whole((2 * tile_rows, NT * BLOCK))],
        out_shape=[
            jax.ShapeDtypeStruct((3, tile_rows, BLOCK), jnp.bfloat16),
            jax.ShapeDtypeStruct((2 * tile_rows, NT * BLOCK), jnp.bfloat16),
        ],
        scratch_shapes=[pltpu.VMEM((tile_rows * NT, BLOCK), jnp.float32)],
        compiler_params=pltpu.CompilerParams(vmem_limit_bytes=16 * 2**20),
    )(tiles)


def take_natural(tiles, tile_rows):
    return pl.pallas_call(
        natural_kernel,
        grid=(NT,),
        in_specs=[pl.BlockSpec((1, NT, tile_rows * BLOCK), lambda t: (t, 0, 0))],
        out_specs=[
            pl.BlockSpec((tile_rows, NT * BLOCK), lambda t: (t, 0)),
            pl.BlockSpec((tile_rows, 2 * BLOCK), lambda t: (t, 0)),
        ],
        out_shape=[
            jax.ShapeDtypeStruct((NT * tile_rows, NT * BLOCK), jnp.bfloat16),
            jax.ShapeDtypeStruct((NT * tile_rows, 2 * BLOCK), jnp.bfloat16),
        ],
        scratch_shapes=[pltpu.VMEM((tile_rows * NT, BLOCK), jnp.float32)],
        compiler_params=pltpu.CompilerParams(vmem_limit_bytes=16 * 2**20),
        cost_estimate=pl.CostEstimate(
            flops=0, bytes_accessed=16 * NT * tile_rows * NT * BLOCK, transcendentals=0
        ),
    )(tiles)


def place_corner(place, slots, which, corner):
    row_index, column_index = place[0], place[1]
    chips, col_count, _, tile_rows, _ = slots[0].shape
    for core, held in enumerate(slots):
        for chip in range(chips):
            first_row = pl.multiple_of((row_index ^ (2 * chip + core)) * tile_rows, tile_rows)
            for col in range(col_count):
                first_col = pl.multiple_of((column_index ^ col) * BLOCK, BLOCK)
                corner[pl.ds(first_row, tile_rows), pl.ds(first_col, BLOCK)] = held[
                    chip, col, which
                ].astype(jnp.float32)


def first_kernel(place, near, far, factor, inverse, rest, work, done):
    place_corner(place, (near, far), 0, rest)
    factor_rest(rest, factor, inverse, work, done)


def second_kernel(
    place, near, far, first_inverse, factor, inverse, cross, rest, work, done
):
    place_corner(place, (near, far), 1, rest)
    solved = exact_dot(rest[...], first_inverse[...], ((1,), (1,))).astype(jnp.bfloat16)
    cross[...] = solved
    place_corner(place, (near, far), 2, rest)
    rest[...] = rest[...] - fast_dot(solved, solved, ((1,), (1,)))
    factor_rest(rest, factor, inverse, work, done)


def factor_call(body, place, slots, extra, extra_out):
    square = jax.ShapeDtypeStruct((P_SIZE, P_SIZE), jnp.float32)
    on_vmem = pl.BlockSpec(memory_space=pltpu.VMEM)
    return pl.pallas_call(
        body,
        in_specs=[pl.BlockSpec(memory_space=pltpu.SMEM)] + [on_vmem] * (2 + len(extra)),
        out_shape=[square, square] + extra_out,
        scratch_shapes=factor_scratch(),
        compiler_params=pltpu.CompilerParams(vmem_limit_bytes=32 * 2**20),
        cost_estimate=pl.CostEstimate(
            flops=20 * 10**9, bytes_accessed=4 * 2**20, transcendentals=0
        ),
    )(place, *slots, *extra)


def split(value):
    high = value.astype(jnp.bfloat16)
    return high, (value - high.astype(jnp.float32)).astype(jnp.bfloat16)


def tail_kernel(pieces, group, *refs):
    place, natural = refs[0], refs[1]
    lefts = refs[2 : 2 + pieces[0]]
    tops = refs[2 + pieces[0] : 2 + pieces[0] + pieces[1]]
    first_factor, first_inverse, second_factor, second_inverse, cross, result = refs[
        2 + sum(pieces) : 8 + sum(pieces)
    ]
    (
        given_cols,
        solved_cols,
        first_high,
        first_low,
        second_high,
        second_low,
        cross_mixed,
        solved_rows,
        copied,
    ) = refs[8 + sum(pieces) :]
    row_index, column_index = place[0], place[1]
    tile_rows = tops[0].shape[0] // 2
    own_row = pl.multiple_of(row_index * tile_rows, tile_rows)
    own_col = pl.multiple_of(column_index * BLOCK, BLOCK)
    order = P_SIZE
    at_group = pl.program_id(0)

    @pl.when(at_group == 0)
    def _():
        copies = []
        for offset, piece in enumerate(tops):
            first_row = pl.multiple_of((row_index ^ offset) * tile_rows, tile_rows)
            for t in range(2):
                copies.append(
                    pltpu.make_async_copy(
                        piece.at[pl.ds(t * tile_rows, tile_rows), :],
                        given_cols.at[pl.ds(t * order + first_row, tile_rows), :],
                        copied.at[2 * offset + t],
                    )
                )
                copies[-1].start()
        first_plain = split(first_inverse[...])
        second_plain = split(second_inverse[...])
        for offset in range(len(lefts)):
            first_col = pl.multiple_of((column_index ^ offset) * BLOCK, BLOCK)
            here = slice(offset * BLOCK, (offset + 1) * BLOCK)
            first_high[:, here], first_low[:, here] = split(
                first_inverse[:, pl.ds(first_col, BLOCK)]
            )
            second_high[:, here], second_low[:, here] = split(
                second_inverse[:, pl.ds(first_col, BLOCK)]
            )
            cross_mixed[here, :] = cross[pl.ds(first_col, BLOCK), :]
        for copy in copies:
            copy.wait()
        for begin in range(2 * BLOCK, NT * BLOCK, 2 * BLOCK):
            here = slice(begin, begin + 2 * BLOCK)
            given = given_cols[0:order, here]
            solved = fast_dot(first_plain[0], given) + fast_dot(first_plain[1], given)
            rounded = solved.astype(jnp.bfloat16)
            solved_cols[0:order, here] = rounded
            left_over = given_cols[order:, here].astype(jnp.float32) - fast_dot(
                cross[...], rounded
            )
            high, low = split(left_over)
            solved = (
                fast_dot(second_plain[0], high)
                + fast_dot(second_plain[0], low)
                + fast_dot(second_plain[1], high)
            )
            solved_cols[order:, here] = solved.astype(jnp.bfloat16)

    across = ((1,), (1,))
    given = jnp.concatenate([left[:, 0:BLOCK] for left in lefts], axis=1)
    solved = fast_dot(given, first_high[...], across) + fast_dot(given, first_low[...], across)
    solved_rows[:, 0:order] = solved
    rounded_first = solved.astype(jnp.bfloat16)
    given = jnp.concatenate([left[:, BLOCK : 2 * BLOCK] for left in lefts], axis=1)
    left_over = given.astype(jnp.float32) - fast_dot(rounded_first, cross_mixed[...], across)
    high, low = split(left_over)
    solved = (
        fast_dot(high, second_high[...], across)
        + fast_dot(low, second_high[...], across)
        + fast_dot(high, second_low[...], across)
    )
    solved_rows[:, order:] = solved
    rounded = jnp.concatenate([rounded_first, solved.astype(jnp.bfloat16)], axis=1)
    for begin in range(2 * BLOCK, NT * BLOCK, 2 * BLOCK):
        here = slice(begin, begin + 2 * BLOCK)
        kept = natural[:, here].astype(jnp.float32) - fast_dot(rounded, solved_cols[:, here])
        for s in (begin // BLOCK, begin // BLOCK + 1):
            for t in range(group):
                result[t, s] = kept[
                    t * tile_rows : (t + 1) * tile_rows,
                    s * BLOCK - begin : (s + 1) * BLOCK - begin,
                ]
    for t in range(group):
        rows = slice(t * tile_rows, (t + 1) * tile_rows)
        result[t, 0] = solved_rows[rows, pl.ds(own_col, BLOCK)]
        result[t, 1] = solved_rows[rows, pl.ds(order + own_col, BLOCK)]

    @pl.when(at_group == 0)
    def _():
        result[0, 0] = first_factor[pl.ds(own_row, tile_rows), pl.ds(own_col, BLOCK)]
        result[1, 1] = second_factor[pl.ds(own_row, tile_rows), pl.ds(own_col, BLOCK)]
        result[0, 1] = jnp.zeros((tile_rows, BLOCK), jnp.float32)
        for t in range(2):
            for s in range(2, NT):
                result[t, s] = jnp.zeros((tile_rows, BLOCK), jnp.float32)


def tail(place, natural, lefts, tops, factors, tile_rows):
    group = 4
    rows = group * tile_rows
    square = whole((P_SIZE, P_SIZE))
    half = pltpu.VMEM((P_SIZE, P_SIZE), jnp.bfloat16)
    return pl.pallas_call(
        functools.partial(tail_kernel, (len(lefts), len(tops)), group),
        grid=(NT // group,),
        in_specs=[
            pl.BlockSpec(memory_space=pltpu.SMEM),
            pl.BlockSpec((rows, NT * BLOCK), lambda i: (i, 0)),
            *[pl.BlockSpec((rows, 2 * BLOCK), lambda i: (i, 0)) for _ in lefts],
            *[pl.BlockSpec(memory_space=pl.ANY) for _ in tops],
            *[square] * 5,
        ],
        out_specs=pl.BlockSpec((group, NT, tile_rows, BLOCK), lambda i: (i, 0, 0, 0)),
        out_shape=jax.ShapeDtypeStruct((NT, NT, tile_rows, BLOCK), jnp.float32),
        scratch_shapes=[
            pltpu.VMEM((2 * P_SIZE, NT * BLOCK), jnp.bfloat16),
            pltpu.VMEM((2 * P_SIZE, NT * BLOCK), jnp.bfloat16),
            *[half] * 5,
            pltpu.VMEM((rows, 2 * P_SIZE), jnp.float32),
            pltpu.SemaphoreType.DMA((2 * len(tops),)),
        ],
        compiler_params=pltpu.CompilerParams(vmem_limit_bytes=56 * 2**20),
    )(place, natural, *lefts, *tops, *factors)


def swap(value, axis, offset):
    count = lax.axis_size(axis)
    return lax.ppermute(value, axis, [(i, i ^ offset) for i in range(count)])


def per_device(kernel):
    row_count = lax.axis_size("row")
    col_count = lax.axis_size("col")
    tile_rows = P_SIZE // row_count
    if P_SIZE != col_count * BLOCK or tile_rows % STEP:
        return per_device_general(kernel)
    place = jnp.stack([lax.axis_index("row"), lax.axis_index("col")]).astype(jnp.int32)
    tiles = kernel.reshape(NT, NT, tile_rows * BLOCK)
    corner, top = take_top(tiles, tile_rows)
    natural, left = take_natural(tiles, tile_rows)
    chips = range(2, row_count, 2)
    over_cols = jnp.stack([corner] + [swap(corner, "col", d) for d in range(1, col_count)])
    near = jnp.stack([over_cols] + [swap(over_cols, "row", d) for d in chips])
    far = swap(near, "row", 1)
    lefts = [left] + [swap(left, "col", d) for d in range(1, col_count)]
    even = [top] + [swap(top, "row", d) for d in chips]
    first_factor, first_inverse = factor_call(first_kernel, place, (near, far), (), [])
    odd = [swap(value, "row", 1) for value in even]
    half = jax.ShapeDtypeStruct((P_SIZE, P_SIZE), jnp.bfloat16)
    second_factor, second_inverse, cross = factor_call(
        second_kernel, place, (near, far), (first_inverse,), [half]
    )
    tops = [value for pair in zip(even, odd) for value in pair]
    factors = (first_factor, first_inverse, second_factor, second_inverse, cross)
    result = tail(place, natural, lefts, tops, factors, tile_rows)
    return result.reshape(kernel.shape)


def solution(mesh):
    placed = P(None, "row", None, "col", None)
    return jax.shard_map(
        per_device, mesh=mesh, in_specs=(placed,), out_specs=placed, check_vma=False
    )
```

profile of v0, /device:TPU:9, one launch (start us, length us, event | category | flops | bytes accessed | tf_op | source)
XLA Modules:
  0.0 117.4 jit_solution(6102836476190113837)
XLA Ops:
  0.0 2.2 %copy-done = bf16[16,1,16,1,8192]{4,2,3,1,0:T(8,128)(2,1)S(1)} copy-done((bf16[16,1,16,1,8192]{4,2,3,1,0:T(8,128)(2,1)S(1)}, bf16[16,1,16,1,8192]{4,2,3,1,0:T(8,128)(2,1)}, u32[]{:S(2)}) %copy-start) | copy-done | bytes 4194328
  2.6 1.4 %collective-permute-start.12 = (bf16[3,64,128]{2,1,0:T(8,128)(2,1)S(1)}, bf16[3,64,128]{2,1,0:T(8,128)(2,1)S(1)}, u32[]{:S(2)}, u32[]{:S(2)}) collective-permute-start(bf16[3,64,128]{2,1,0:T(8,128)(2,1)S(1)} %get-tuple-element.17), channel_id=1, source_target_pairs={{0,3},{1,2},{2,1},{3,0},{4,7},{5,6},{6,5},{7,4},{8,11},{9,10},{10,... | collective-permute-start | bytes 147464 | tf_op jit(solution)/shard_map/ppermute | solution.py:456
  4.0 1.1 collective-permute-start.11
  5.1 1.1 collective-permute-start.10
  6.2 1.7 %collective-permute-done.11 = bf16[3,64,128]{2,1,0:T(8,128)(2,1)S(1)} collective-permute-done((bf16[3,64,128]{2,1,0:T(8,128)(2,1)S(1)}, bf16[3,64,128]{2,1,0:T(8,128)(2,1)S(1)}, u32[]{:S(2)}, u32[]{:S(2)}) %collective-permute-start.11) | collective-permute-done | bytes 49184 | tf_op jit(solution)/shard_map/ppermute | solution.py:456
  7.9 1.6 %collective-permute-done.10 = bf16[3,64,128]{2,1,0:T(8,128)(2,1)S(1)} collective-permute-done((bf16[3,64,128]{2,1,0:T(8,128)(2,1)S(1)}, bf16[3,64,128]{2,1,0:T(8,128)(2,1)S(1)}, u32[]{:S(2)}, u32[]{:S(2)}) %collective-permute-start.10) | collective-permute-done | bytes 49184 | tf_op jit(solution)/shard_map/ppermute | solution.py:456
  9.5 1.3 %collective-permute-start.14 = (bf16[4,3,64,128]{3,2,1,0:T(8,128)(2,1)S(1)}, bf16[4,3,64,128]{3,2,1,0:T(8,128)(2,1)S(1)}, u32[]{:S(2)}, u32[]{:S(2)}) collective-permute-start(bf16[4,3,64,128]{3,2,1,0:T(8,128)(2,1)S(1)} %get-tuple-element.24), channel_id=1, source_target_pairs={{0,16},{4,20},{8,24},{12,28},{16,0},{20,4},{24,8},{28,12},{1,17},{... | collective-permute-start | bytes 589832 | tf_op jit(solution)/shard_map/ppermute | solution.py:456
  10.8 1.2 %collective-permute-start.13 = (bf16[4,3,64,128]{3,2,1,0:T(8,128)(2,1)S(1)}, bf16[4,3,64,128]{3,2,1,0:T(8,128)(2,1)S(1)}, u32[]{:S(2)}, u32[]{:S(2)}) collective-permute-start(bf16[4,3,64,128]{3,2,1,0:T(8,128)(2,1)S(1)} %get-tuple-element.24), channel_id=1, source_target_pairs={{0,8},{4,12},{8,0},{12,4},{16,24},{20,28},{24,16},{28,20},{1,9},{5... | collective-permute-start | bytes 589832 | tf_op jit(solution)/shard_map/ppermute | solution.py:456
  12.3 2.2 %collective-permute-done.14 = bf16[4,3,64,128]{3,2,1,0:T(8,128)(2,1)S(1)} collective-permute-done((bf16[4,3,64,128]{3,2,1,0:T(8,128)(2,1)S(1)}, bf16[4,3,64,128]{3,2,1,0:T(8,128)(2,1)S(1)}, u32[]{:S(2)}, u32[]{:S(2)}) %collective-permute-start.14) | collective-permute-done | bytes 196640 | tf_op jit(solution)/shard_map/ppermute | solution.py:456
  14.5 1.2 collective-permute-done.13
  15.7 3.8 %collective-permute-done.15 = bf16[4,3,64,128]{3,2,1,0:T(8,128)(2,1)S(1)} collective-permute-done((bf16[4,3,64,128]{3,2,1,0:T(8,128)(2,1)S(1)}, bf16[4,3,64,128]{3,2,1,0:T(8,128)(2,1)S(1)}, u32[]{:S(2)}, u32[]{:S(2)}) %collective-permute-start.15) | collective-permute-done | bytes 196640 | tf_op jit(solution)/shard_map/ppermute | solution.py:456
  19.6 2.9 %collective-permute-start.16 = (bf16[4,4,3,64,128]{4,3,2,1,0:T(8,128)(2,1)S(1)}, bf16[4,4,3,64,128]{4,3,2,1,0:T(8,128)(2,1)S(1)}, u32[]{:S(2)}, u32[]{:S(2)}) collective-permute-start(bf16[4,4,3,64,128]{4,3,2,1,0:T(8,128)(2,1)S(1)} %pad_maximum_fusion.near), channel_id=1, source_target_pairs={{0,4},{4,0},{8,12},{12,8},{16,20},{20,16},{24,28},{28,24},{1,5},{5... | collective-permute-start | bytes 2359304 | tf_op jit(solution)/shard_map/ppermute | solution.py:456
  22.6 2.1 %collective-permute-start.8 = (bf16[128,2048]{1,0:T(8,128)(2,1)S(1)}, bf16[128,2048]{1,0:T(8,128)(2,1)S(1)}, u32[]{:S(2)}, u32[]{:S(2)}) collective-permute-start(bf16[128,2048]{1,0:T(8,128)(2,1)S(1)} %get-tuple-element.16.refs_6_), channel_id=1, source_target_pairs={{0,24},{4,28},{8,16},{12,20},{16,8},{20,12},{24,0},{28,4},{1,25},{... | collective-permute-start | bytes 1572872 | tf_op jit(solution)/shard_map/ppermute | solution.py:456
  26.1 3.5 %shard_map.17 = (bf16[1024,2048]{1,0:T(8,128)(2,1)S(1)}, bf16[1024,256]{1,0:T(8,128)(2,1)S(1)}) custom-call(bf16[16,16,8192]{2,1,0:T(8,128)(2,1)S(1)} %bitcast.14), custom_call_target="tpu_custom_call" | custom-call | bytes 33554432 | tf_op jit(solution)/shard_map/pallas_call | solution.py:248
  29.6 2.0 %copy-done.1 = bf16[1024,2048]{1,0:T(8,128)(2,1)} copy-done((bf16[1024,2048]{1,0:T(8,128)(2,1)}, bf16[1024,2048]{1,0:T(8,128)(2,1)S(1)}, u32[]{:S(2)}) %copy-start.1) | copy-done | bytes 4194328
  32.5 18.1 %shard_map.19 = (f32[512,512]{1,0:T(8,128)S(1)}, f32[512,512]{1,0:T(8,128)S(1)}) custom-call(s32[2]{0:T(128)S(1)} %pad_add_fusion.place.refs_0_, bf16[4,4,3,64,128]{4,3,2,1,0:T(8,128)(2,1)S(1)} %pad_maximum_fusion.near, bf16[4,4,3,64,128]{4,3,2,1,0:T(8,128)(2,1)S(1)} %collective-permute-done.16.far), custom_call_target="tpu_custom_call" | custom-call | flops 20000000000 | bytes 4194304 | tf_op jit(solution)/shard_map/pallas_call | solution.py:300
  50.6 1.0 copy-done.2
  51.7 2.3 %collective-permute-start.1 = (bf16[1024,256]{1,0:T(8,128)(2,1)S(1)}, bf16[1024,256]{1,0:T(8,128)(2,1)S(1)}, u32[]{:S(2)}, u32[]{:S(2)}) collective-permute-start(bf16[1024,256]{1,0:T(8,128)(2,1)S(1)} %get-tuple-element.15.refs_2_), channel_id=1, source_target_pairs={{0,2},{1,3},{2,0},{3,1},{4,6},{5,7},{6,4},{7,5},{8,10},{9,11},{10,... | collective-permute-start | bytes 1572872 | tf_op jit(solution)/shard_map/ppermute | solution.py:456
  54.7 13.0 %collective-permute-done.2.refs_5_ = bf16[1024,256]{1,0:T(8,128)(2,1)S(1)} collective-permute-done((bf16[1024,256]{1,0:T(8,128)(2,1)S(1)}, bf16[1024,256]{1,0:T(8,128)(2,1)S(1)}, u32[]{:S(2)}, u32[]{:S(2)}) %collective-permute-start.2) | collective-permute-done | bytes 524320 | tf_op jit(solution)/shard_map/ppermute | solution.py:456
  67.7 1.2 collective-permute-start.5
  68.9 20.6 %shard_map.20 = (f32[512,512]{1,0:T(8,128)S(1)}, f32[512,512]{1,0:T(8,128)S(1)}, bf16[512,512]{1,0:T(8,128)(2,1)S(1)}) custom-call(s32[2]{0:T(128)S(1)} %pad_add_fusion.place.refs_0_, bf16[4,4,3,64,128]{4,3,2,1,0:T(8,128)(2,1)S(1)} %pad_maximum_fusion.near, bf16[4,4,3,64,128]{4,3,2,1,0:T(8,128)(2,1)S(1)} %collective-permute-done.16.far, ...), custom_call_target="tpu_custom_call" | custom-call | flops 20000000000 | bytes 4194304 | tf_op jit(solution)/shard_map/pallas_call | solution.py:300
  89.5 1.0 copy-done.4
  90.5 1.1 copy-done.5
  93.9 23.3 %shard_map.21 = f32[16,16,64,128]{3,2,1,0:T(8,128)} custom-call(s32[2]{0:T(128)} %copy-done.9, bf16[1024,2048]{1,0:T(8,128)(2,1)} %copy-done.1, bf16[1024,256]{1,0:T(8,128)(2,1)} %copy-done.7, bf16[1024,256]{1,0:T(8,128)(2,1)} %copy-done.13, bf16[1024,256]{1,0:T(8,128)(2,1)} %copy-done.12, bf16[1024,256]{1,0:T(8,128)(2,1)} %copy-done.11, ...), custom_call_target="tpu_custom_call" | custom-call | tf_op jit(solution)/shard_map/pallas_call | solution.py:431
  (52 shorter events, 6.2 us)
Async XLA Ops:
  0.0 2.2 %copy-start = (bf16[16,1,16,1,8192]{4,2,3,1,0:T(8,128)(2,1)S(1)}, bf16[16,1,16,1,8192]{4,2,3,1,0:T(8,128)(2,1)}, u32[]{:S(2)}) copy-start(bf16[16,1,16,1,8192]{4,2,3,1,0:T(8,128)(2,1)} %param.1) | copy-start | bytes 12582916
  2.6 48.0 %copy-start.6 = (bf16[128,2048]{1,0:T(8,128)(2,1)}, bf16[128,2048]{1,0:T(8,128)(2,1)S(1)}, u32[]{:S(2)}) copy-start(bf16[128,2048]{1,0:T(8,128)(2,1)S(1)} %get-tuple-element.16.refs_6_) | copy-start | bytes 1572868
  2.6 3.6 %collective-permute-start.12 = (bf16[3,64,128]{2,1,0:T(8,128)(2,1)S(1)}, bf16[3,64,128]{2,1,0:T(8,128)(2,1)S(1)}, u32[]{:S(2)}, u32[]{:S(2)}) collective-permute-start(bf16[3,64,128]{2,1,0:T(8,128)(2,1)S(1)} %get-tuple-element.17), channel_id=1, source_target_pairs={{0,3},{1,2},{2,1},{3,0},{4,7},{5,6},{6,5},{7,4},{8,11},{9,10},{10,... | collective-permute-start | bytes 147464 | tf_op jit(solution)/shard_map/ppermute | solution.py:456
  4.0 3.9 %collective-permute-start.11 = (bf16[3,64,128]{2,1,0:T(8,128)(2,1)S(1)}, bf16[3,64,128]{2,1,0:T(8,128)(2,1)S(1)}, u32[]{:S(2)}, u32[]{:S(2)}) collective-permute-start(bf16[3,64,128]{2,1,0:T(8,128)(2,1)S(1)} %get-tuple-element.17), channel_id=1, source_target_pairs={{0,2},{1,3},{2,0},{3,1},{4,6},{5,7},{6,4},{7,5},{8,10},{9,11},{10,... | collective-permute-start | bytes 147464 | tf_op jit(solution)/shard_map/ppermute | solution.py:456
  5.1 4.4 %collective-permute-start.10 = (bf16[3,64,128]{2,1,0:T(8,128)(2,1)S(1)}, bf16[3,64,128]{2,1,0:T(8,128)(2,1)S(1)}, u32[]{:S(2)}, u32[]{:S(2)}) collective-permute-start(bf16[3,64,128]{2,1,0:T(8,128)(2,1)S(1)} %get-tuple-element.17), channel_id=1, source_target_pairs={{0,1},{1,0},{2,3},{3,2},{4,5},{5,4},{6,7},{7,6},{8,9},{9,8},{10,11... | collective-permute-start | bytes 147464 | tf_op jit(solution)/shard_map/ppermute | solution.py:456
  9.5 5.0 %collective-permute-start.14 = (bf16[4,3,64,128]{3,2,1,0:T(8,128)(2,1)S(1)}, bf16[4,3,64,128]{3,2,1,0:T(8,128)(2,1)S(1)}, u32[]{:S(2)}, u32[]{:S(2)}) collective-permute-start(bf16[4,3,64,128]{3,2,1,0:T(8,128)(2,1)S(1)} %get-tuple-element.24), channel_id=1, source_target_pairs={{0,16},{4,20},{8,24},{12,28},{16,0},{20,4},{24,8},{28,12},{1,17},{... | collective-permute-start | bytes 589832 | tf_op jit(solution)/shard_map/ppermute | solution.py:456
  10.8 4.8 %collective-permute-start.13 = (bf16[4,3,64,128]{3,2,1,0:T(8,128)(2,1)S(1)}, bf16[4,3,64,128]{3,2,1,0:T(8,128)(2,1)S(1)}, u32[]{:S(2)}, u32[]{:S(2)}) collective-permute-start(bf16[4,3,64,128]{3,2,1,0:T(8,128)(2,1)S(1)} %get-tuple-element.24), channel_id=1, source_target_pairs={{0,8},{4,12},{8,0},{12,4},{16,24},{20,28},{24,16},{28,20},{1,9},{5... | collective-permute-start | bytes 589832 | tf_op jit(solution)/shard_map/ppermute | solution.py:456
  12.1 7.4 %collective-permute-start.15 = (bf16[4,3,64,128]{3,2,1,0:T(8,128)(2,1)S(1)}, bf16[4,3,64,128]{3,2,1,0:T(8,128)(2,1)S(1)}, u32[]{:S(2)}, u32[]{:S(2)}) collective-permute-start(bf16[4,3,64,128]{3,2,1,0:T(8,128)(2,1)S(1)} %get-tuple-element.24), channel_id=1, source_target_pairs={{0,24},{4,28},{8,16},{12,20},{16,8},{20,12},{24,0},{28,4},{1,25},{... | collective-permute-start | bytes 589832 | tf_op jit(solution)/shard_map/ppermute | solution.py:456
  19.6 12.0 %collective-permute-start.16 = (bf16[4,4,3,64,128]{4,3,2,1,0:T(8,128)(2,1)S(1)}, bf16[4,4,3,64,128]{4,3,2,1,0:T(8,128)(2,1)S(1)}, u32[]{:S(2)}, u32[]{:S(2)}) collective-permute-start(bf16[4,4,3,64,128]{4,3,2,1,0:T(8,128)(2,1)S(1)} %pad_maximum_fusion.near), channel_id=1, source_target_pairs={{0,4},{4,0},{8,12},{12,8},{16,20},{20,16},{24,28},{28,24},{1,5},{5... | collective-permute-start | bytes 2359304 | tf_op jit(solution)/shard_map/ppermute | solution.py:456
  22.6 29.1 %collective-permute-start.8 = (bf16[128,2048]{1,0:T(8,128)(2,1)S(1)}, bf16[128,2048]{1,0:T(8,128)(2,1)S(1)}, u32[]{:S(2)}, u32[]{:S(2)}) collective-permute-start(bf16[128,2048]{1,0:T(8,128)(2,1)S(1)} %get-tuple-element.16.refs_6_), channel_id=1, source_target_pairs={{0,24},{4,28},{8,16},{12,20},{16,8},{20,12},{24,0},{28,4},{1,25},{... | collective-permute-start | bytes 1572872 | tf_op jit(solution)/shard_map/ppermute | solution.py:456
  24.7 29.3 %collective-permute-start.6 = (bf16[128,2048]{1,0:T(8,128)(2,1)S(1)}, bf16[128,2048]{1,0:T(8,128)(2,1)}, u32[]{:S(2)}, u32[]{:S(2)}) collective-permute-start(bf16[128,2048]{1,0:T(8,128)(2,1)S(1)} %get-tuple-element.16.refs_6_), channel_id=1, source_target_pairs={{0,16},{4,20},{8,24},{12,28},{16,0},{20,4},{24,8},{28,12},{1,17},{... | collective-permute-start | bytes 1572872 | tf_op jit(solution)/shard_map/ppermute | solution.py:456
  24.9 29.1 %collective-permute-start.4 = (bf16[128,2048]{1,0:T(8,128)(2,1)S(1)}, bf16[128,2048]{1,0:T(8,128)(2,1)}, u32[]{:S(2)}, u32[]{:S(2)}) collective-permute-start(bf16[128,2048]{1,0:T(8,128)(2,1)S(1)} %get-tuple-element.16.refs_6_), channel_id=1, source_target_pairs={{0,8},{4,12},{8,0},{12,4},{16,24},{20,28},{24,16},{28,20},{1,9},{5... | collective-permute-start | bytes 1572872 | tf_op jit(solution)/shard_map/ppermute | solution.py:456
  25.2 29.4 %collective-permute-start.3 = (bf16[128,2048]{1,0:T(8,128)(2,1)S(1)}, bf16[128,2048]{1,0:T(8,128)(2,1)}, u32[]{:S(2)}, u32[]{:S(2)}) collective-permute-start(bf16[128,2048]{1,0:T(8,128)(2,1)S(1)} %get-tuple-element.16.refs_6_), channel_id=1, source_target_pairs={{0,4},{4,0},{8,12},{12,8},{16,20},{20,16},{24,28},{28,24},{1,5},{5... | collective-permute-start | bytes 1572872 | tf_op jit(solution)/shard_map/ppermute | solution.py:456
  31.6 22.4 %copy-start.7 = (bf16[1024,256]{1,0:T(8,128)(2,1)}, bf16[1024,256]{1,0:T(8,128)(2,1)S(1)}, u32[]{:S(2)}) copy-start(bf16[1024,256]{1,0:T(8,128)(2,1)S(1)} %get-tuple-element.15.refs_2_) | copy-start | bytes 1572868
  31.6 37.2 %copy-start.9 = (s32[2]{0:T(128)}, s32[2]{0:T(128)S(1)}, u32[]{:S(2)}) copy-start(s32[2]{0:T(128)S(1)} %pad_add_fusion.place.refs_0_) | copy-start | bytes 28
  31.6 36.0 %collective-permute-start.2 = (bf16[1024,256]{1,0:T(8,128)(2,1)S(1)}, bf16[1024,256]{1,0:T(8,128)(2,1)S(1)}, u32[]{:S(2)}, u32[]{:S(2)}) collective-permute-start(bf16[1024,256]{1,0:T(8,128)(2,1)S(1)} %get-tuple-element.15.refs_2_), channel_id=1, source_target_pairs={{0,3},{1,2},{2,1},{3,0},{4,7},{5,6},{6,5},{7,4},{8,11},{9,10},{10,... | collective-permute-start | bytes 1572872 | tf_op jit(solution)/shard_map/ppermute | solution.py:456
  51.6 37.8 %copy-start.3 = (f32[512,512]{1,0:T(8,128)}, f32[512,512]{1,0:T(8,128)S(1)}, u32[]{:S(2)}) copy-start(f32[512,512]{1,0:T(8,128)S(1)} %get-tuple-element.19.first_inverse.refs_15_) | copy-start | bytes 3145732
  51.7 37.8 %copy-start.10 = (bf16[128,2048]{1,0:T(8,128)(2,1)}, bf16[128,2048]{1,0:T(8,128)(2,1)S(1)}, u32[]{:S(2)}) copy-start(bf16[128,2048]{1,0:T(8,128)(2,1)S(1)} %collective-permute-done.8.refs_12_) | copy-start | bytes 1572868
  51.7 40.7 %collective-permute-start.1 = (bf16[1024,256]{1,0:T(8,128)(2,1)S(1)}, bf16[1024,256]{1,0:T(8,128)(2,1)S(1)}, u32[]{:S(2)}, u32[]{:S(2)}) collective-permute-start(bf16[1024,256]{1,0:T(8,128)(2,1)S(1)} %get-tuple-element.15.refs_2_), channel_id=1, source_target_pairs={{0,2},{1,3},{2,0},{3,1},{4,6},{5,7},{6,4},{7,5},{8,10},{9,11},{10,... | collective-permute-start | bytes 1572872 | tf_op jit(solution)/shard_map/ppermute | solution.py:456
  54.0 38.4 %collective-permute-start = (bf16[1024,256]{1,0:T(8,128)(2,1)S(1)}, bf16[1024,256]{1,0:T(8,128)(2,1)S(1)}, u32[]{:S(2)}, u32[]{:S(2)}) collective-permute-start(bf16[1024,256]{1,0:T(8,128)(2,1)S(1)} %get-tuple-element.15.refs_2_), channel_id=1, source_target_pairs={{0,1},{1,0},{2,3},{3,2},{4,5},{5,4},{6,7},{7,6},{8,9},{9,8},{10,11... | collective-permute-start | bytes 1572872 | tf_op jit(solution)/shard_map/ppermute | solution.py:456
  54.0 38.4 %collective-permute-start.9 = (bf16[128,2048]{1,0:T(8,128)(2,1)S(1)}, bf16[128,2048]{1,0:T(8,128)(2,1)S(1)}, u32[]{:S(2)}, u32[]{:S(2)}) collective-permute-start(bf16[128,2048]{1,0:T(8,128)(2,1)S(1)} %collective-permute-done.8.refs_12_), channel_id=1, source_target_pairs={{0,4},{4,0},{8,12},{12,8},{16,20},{20,16},{24,28},{28,24},{1,5},{5... | collective-permute-start | bytes 1572872 | tf_op jit(solution)/shard_map/ppermute | solution.py:456
  54.6 37.8 %collective-permute-start.7 = (bf16[128,2048]{1,0:T(8,128)(2,1)}, bf16[128,2048]{1,0:T(8,128)(2,1)S(1)}, u32[]{:S(2)}, u32[]{:S(2)}) collective-permute-start(bf16[128,2048]{1,0:T(8,128)(2,1)} %collective-permute-done.6.refs_10_), channel_id=1, source_target_pairs={{0,4},{4,0},{8,12},{12,8},{16,20},{20,16},{24,28},{28,24},{1,5},{5... | collective-permute-start | bytes 1572872 | tf_op jit(solution)/shard_map/ppermute | solution.py:456
  67.7 21.8 %copy-start.11 = (bf16[1024,256]{1,0:T(8,128)(2,1)}, bf16[1024,256]{1,0:T(8,128)(2,1)S(1)}, u32[]{:S(2)}) copy-start(bf16[1024,256]{1,0:T(8,128)(2,1)S(1)} %collective-permute-done.2.refs_5_) | copy-start | bytes 1572868
  67.7 24.7 %collective-permute-start.5 = (bf16[128,2048]{1,0:T(8,128)(2,1)}, bf16[128,2048]{1,0:T(8,128)(2,1)S(1)}, u32[]{:S(2)}, u32[]{:S(2)}) collective-permute-start(bf16[128,2048]{1,0:T(8,128)(2,1)} %collective-permute-done.4.refs_8_), channel_id=1, source_target_pairs={{0,4},{4,0},{8,12},{12,8},{16,20},{20,16},{24,28},{28,24},{1,5},{5... | collective-permute-start | bytes 1572872 | tf_op jit(solution)/shard_map/ppermute | solution.py:456
  (10 other events, 11.6 us)
where the time goes:
time: 118 us; the launch traced here: 117 us
  Pallas kernels  65.9 us (56%)
  waiting for transfers between devices  23.6 us (20%)
  starting transfers between devices  17.8 us (15%)
  local copies, waits for them, and re-layouts  9.51 us (8%)
    pallas_call x2, Pallas kernels, factor_call(): pl.pallas_call(body, in_specs=[pl.BlockSpec(memory_space=pltpu.SMEM)] + [...  38.8 us
    ppermute x17, waiting for transfers between devices, swap(): return lax.ppermute(value, axis, [(i, i ^ offset) for i in range(count)])  23.6 us
    pallas_call x1, Pallas kernels, tail(): pl.pallas_call(functools.partial(tail_kernel, (len(lefts), len(tops)), gr...  23.3 us
    ppermute x17, starting transfers between devices, swap(): return lax.ppermute(value, axis, [(i, i ^ offset) for i in range(count)])  17.8 us
    unnamed x34, local copies, waits for them, and re-layouts  9.51 us
    pallas_call x1, Pallas kernels, take_natural(): pl.pallas_call(natural_kernel, grid=(NT,), in_specs=[pl.BlockSpec((1, NT,...  3.47 us
  transfers between devices with their start and end apart: 17, of which 6 were waited for; matrix products, arithmetic and copies ran while one was open for 0% of the time, Pallas kernels for 36%

commit v1 on v0

--- a/solution.py
+++ b/solution.py
@@ -24,10 +24,32 @@
     )
 
 
+def split(value):
+    high = value.astype(jnp.bfloat16)
+    return high, (value - high.astype(jnp.float32)).astype(jnp.bfloat16)
+
+
+def split_three(value):
+    high = value.astype(jnp.bfloat16)
+    value = value - high.astype(jnp.float32)
+    return high, *split(value)
+
+
 def fast_dot(left_side, right_side, contract=((1,), (0,))):
     return lax.dot_general(
         left_side, right_side, (contract, ((), ())), preferred_element_type=jnp.float32
     )
+
+
+def repeat_columns(rows, start):
+    slot = lax.broadcasted_iota(jnp.int32, rows.shape, 1) // STEP
+    spread_out = rows if start == 0 else pltpu.roll(rows, BLOCK - start, 1)
+    at_start = spread_out
+    for place in range(1, 6):
+        spread_out = jnp.where(slot == place, pltpu.roll(at_start, place * STEP, 1), spread_out)
+    high, middle, low = (part.astype(jnp.float32) for part in split_three(spread_out))
+    parts = jnp.where(slot < 3, high, jnp.where(slot < 5, middle, low))
+    return jnp.where(slot < 6, parts, 0.0).astype(jnp.bfloat16)
 
 
 def factor_block(work, done):
@@ -39,7 +61,8 @@
             jnp.broadcast_to(halves[0][:, start + j : start + j + 1], (STEP, BLOCK))
             for j in range(STEP)
         ]
-        raw = work[start + STEP :, here] if start + STEP < BLOCK else None
+        if start + STEP < BLOCK:
+            raw = repeat_columns(work[start + STEP :, 0:BLOCK], start)
         kept = [jnp.zeros((STEP, BLOCK), jnp.float32)] * 2
         pivots = jnp.ones((STEP, BLOCK), jnp.float32)
         for k in range(STEP):
@@ -57,9 +80,13 @@
         inverse = 1.0 / pivots
         for h in range(2):
             done[here, h * BLOCK : (h + 1) * BLOCK] = kept[h] * scale
-        if raw is not None:
+        if start + STEP < BLOCK:
             solved = jnp.concatenate([halves[0] * inverse, halves[1] * inverse], axis=1)
-            work[start + STEP :, :] = work[start + STEP :, :] - exact_dot(raw, solved)
+            high, middle, low = split_three(solved)
+            parts = jnp.concatenate(
+                [high, middle, low, high, middle, high, jnp.zeros_like(high), jnp.zeros_like(high)]
+            )
+            work[start + STEP :, :] = work[start + STEP :, :] - fast_dot(raw, parts)
 
 
 def factor_kernel(given, factor, inverse, rest, work, done):
@@ -286,10 +313,16 @@
 def second_kernel(
     place, near, far, first_inverse, factor, inverse, cross, rest, work, done
 ):
+    place_corner(place, (near, far), 0, rest)
+    given = rest[...].astype(jnp.bfloat16)
+    high, low = split(first_inverse[...])
+    solved = fast_dot(
+        jnp.concatenate([given, given], axis=1),
+        jnp.concatenate([high, low], axis=1),
+        ((1,), (1,)),
+    ).astype(jnp.bfloat16)
+    cross[...] = solved
     place_corner(place, (near, far), 1, rest)
-    solved = exact_dot(rest[...], first_inverse[...], ((1,), (1,))).astype(jnp.bfloat16)
-    cross[...] = solved
-    place_corner(place, (near, far), 2, rest)
     rest[...] = rest[...] - fast_dot(solved, solved, ((1,), (1,)))
     factor_rest(rest, factor, inverse, work, done)
 
@@ -309,151 +342,199 @@
     )(place, *slots, *extra)
 
 
-def split(value):
-    high = value.astype(jnp.bfloat16)
-    return high, (value - high.astype(jnp.float32)).astype(jnp.bfloat16)
-
-
-def tail_kernel(pieces, group, *refs):
-    place, natural = refs[0], refs[1]
-    lefts = refs[2 : 2 + pieces[0]]
-    tops = refs[2 + pieces[0] : 2 + pieces[0] + pieces[1]]
-    first_factor, first_inverse, second_factor, second_inverse, cross, result = refs[
-        2 + sum(pieces) : 8 + sum(pieces)
-    ]
-    (
-        given_cols,
-        solved_cols,
-        first_high,
-        first_low,
-        second_high,
-        second_low,
-        cross_mixed,
-        solved_rows,
-        copied,
-    ) = refs[8 + sum(pieces) :]
-    row_index, column_index = place[0], place[1]
-    tile_rows = tops[0].shape[0] // 2
-    own_row = pl.multiple_of(row_index * tile_rows, tile_rows)
+def rows_kernel(place, *refs):
+    lefts = refs[:-9]
+    first_inverse, second_inverse, cross, rounded, own, *scratch = refs[-9:]
+    first_side, cross_side, second_side, solved_rows = scratch
+    column_index = place[1]
     own_col = pl.multiple_of(column_index * BLOCK, BLOCK)
     order = P_SIZE
-    at_group = pl.program_id(0)
-
-    @pl.when(at_group == 0)
+
+    @pl.when(pl.program_id(0) == 0)
     def _():
-        copies = []
-        for offset, piece in enumerate(tops):
-            first_row = pl.multiple_of((row_index ^ offset) * tile_rows, tile_rows)
-            for t in range(2):
-                copies.append(
-                    pltpu.make_async_copy(
-                        piece.at[pl.ds(t * tile_rows, tile_rows), :],
-                        given_cols.at[pl.ds(t * order + first_row, tile_rows), :],
-                        copied.at[2 * offset + t],
-                    )
-                )
-                copies[-1].start()
-        first_plain = split(first_inverse[...])
-        second_plain = split(second_inverse[...])
         for offset in range(len(lefts)):
-            first_col = pl.multiple_of((column_index ^ offset) * BLOCK, BLOCK)
-            here = slice(offset * BLOCK, (offset + 1) * BLOCK)
-            first_high[:, here], first_low[:, here] = split(
-                first_inverse[:, pl.ds(first_col, BLOCK)]
-            )
-            second_high[:, here], second_low[:, here] = split(
-                second_inverse[:, pl.ds(first_col, BLOCK)]
-            )
-            cross_mixed[here, :] = cross[pl.ds(first_col, BLOCK), :]
-        for copy in copies:
-            copy.wait()
-        for begin in range(2 * BLOCK, NT * BLOCK, 2 * BLOCK):
-            here = slice(begin, begin + 2 * BLOCK)
-            given = given_cols[0:order, here]
-            solved = fast_dot(first_plain[0], given) + fast_dot(first_plain[1], given)
-            rounded = solved.astype(jnp.bfloat16)
-            solved_cols[0:order, here] = rounded
-            left_over = given_cols[order:, here].astype(jnp.float32) - fast_dot(
-                cross[...], rounded
-            )
-            high, low = split(left_over)
-            solved = (
-                fast_dot(second_plain[0], high)
-                + fast_dot(second_plain[0], low)
-                + fast_dot(second_plain[1], high)
-            )
-            solved_cols[order:, here] = solved.astype(jnp.bfloat16)
-
-    across = ((1,), (1,))
-    given = jnp.concatenate([left[:, 0:BLOCK] for left in lefts], axis=1)
-    solved = fast_dot(given, first_high[...], across) + fast_dot(given, first_low[...], across)
+            first = pl.multiple_of((column_index ^ offset) * BLOCK, BLOCK)
+            here = pl.ds(first, BLOCK)
+            for k in range(3):
+                to = slice(k * order + offset * BLOCK, k * order + (offset + 1) * BLOCK)
+                if k < 2:
+                    first_side[to, :] = split(first_inverse[:, here].T)[k]
+                second_side[to, :] = split(second_inverse[:, here].T)[k // 2]
+            to = slice(offset * BLOCK, (offset + 1) * BLOCK)
+            cross_side[:, to] = cross[here, :].astype(jnp.float32).T.astype(jnp.bfloat16)
+
+    given = [left[:, 0:BLOCK] for left in lefts]
+    solved = fast_dot(jnp.concatenate(given + given, axis=1), first_side[...])
     solved_rows[:, 0:order] = solved
-    rounded_first = solved.astype(jnp.bfloat16)
+    first_rounded = solved.astype(jnp.bfloat16)
     given = jnp.concatenate([left[:, BLOCK : 2 * BLOCK] for left in lefts], axis=1)
-    left_over = given.astype(jnp.float32) - fast_dot(rounded_first, cross_mixed[...], across)
+    left_over = given.astype(jnp.float32) - fast_dot(first_rounded, cross_side[...])
     high, low = split(left_over)
-    solved = (
-        fast_dot(high, second_high[...], across)
-        + fast_dot(low, second_high[...], across)
-        + fast_dot(high, second_low[...], across)
-    )
+    solved = fast_dot(jnp.concatenate([high, low, high], axis=1), second_side[...])
     solved_rows[:, order:] = solved
-    rounded = jnp.concatenate([rounded_first, solved.astype(jnp.bfloat16)], axis=1)
-    for begin in range(2 * BLOCK, NT * BLOCK, 2 * BLOCK):
-        here = slice(begin, begin + 2 * BLOCK)
-        kept = natural[:, here].astype(jnp.float32) - fast_dot(rounded, solved_cols[:, here])
-        for s in (begin // BLOCK, begin // BLOCK + 1):
-            for t in range(group):
-                result[t, s] = kept[
-                    t * tile_rows : (t + 1) * tile_rows,
-                    s * BLOCK - begin : (s + 1) * BLOCK - begin,
-                ]
-    for t in range(group):
-        rows = slice(t * tile_rows, (t + 1) * tile_rows)
-        result[t, 0] = solved_rows[rows, pl.ds(own_col, BLOCK)]
-        result[t, 1] = solved_rows[rows, pl.ds(order + own_col, BLOCK)]
-
-    @pl.when(at_group == 0)
-    def _():
-        result[0, 0] = first_factor[pl.ds(own_row, tile_rows), pl.ds(own_col, BLOCK)]
-        result[1, 1] = second_factor[pl.ds(own_row, tile_rows), pl.ds(own_col, BLOCK)]
-        result[0, 1] = jnp.zeros((tile_rows, BLOCK), jnp.float32)
-        for t in range(2):
-            for s in range(2, NT):
-                result[t, s] = jnp.zeros((tile_rows, BLOCK), jnp.float32)
-
-
-def tail(place, natural, lefts, tops, factors, tile_rows):
-    group = 4
-    rows = group * tile_rows
+    rounded[:, 0:order] = first_rounded
+    rounded[:, order:] = solved.astype(jnp.bfloat16)
+    own[:, 0:BLOCK] = solved_rows[:, pl.ds(own_col, BLOCK)]
+    own[:, BLOCK:] = solved_rows[:, pl.ds(order + own_col, BLOCK)]
+
+
+def solve_rows(place, lefts, first_inverse, second_inverse, cross):
+    count = lefts[0].shape[0]
+    rows = count // 2
     square = whole((P_SIZE, P_SIZE))
-    half = pltpu.VMEM((P_SIZE, P_SIZE), jnp.bfloat16)
     return pl.pallas_call(
-        functools.partial(tail_kernel, (len(lefts), len(tops)), group),
-        grid=(NT // group,),
+        rows_kernel,
+        grid=(count // rows,),
         in_specs=[
             pl.BlockSpec(memory_space=pltpu.SMEM),
-            pl.BlockSpec((rows, NT * BLOCK), lambda i: (i, 0)),
             *[pl.BlockSpec((rows, 2 * BLOCK), lambda i: (i, 0)) for _ in lefts],
-            *[pl.BlockSpec(memory_space=pl.ANY) for _ in tops],
+            *[square] * 3,
+        ],
+        out_specs=[
+            pl.BlockSpec((rows, 2 * P_SIZE), lambda i: (i, 0)),
+            pl.BlockSpec((rows, 2 * BLOCK), lambda i: (i, 0)),
+        ],
+        out_shape=[
+            jax.ShapeDtypeStruct((count, 2 * P_SIZE), jnp.bfloat16),
+            jax.ShapeDtypeStruct((count, 2 * BLOCK), jnp.float32),
+        ],
+        scratch_shapes=[
+            pltpu.VMEM((2 * P_SIZE, P_SIZE), jnp.bfloat16),
+            pltpu.VMEM((P_SIZE, P_SIZE), jnp.bfloat16),
+            pltpu.VMEM((3 * P_SIZE, P_SIZE), jnp.bfloat16),
+            pltpu.VMEM((rows, 2 * P_SIZE), jnp.float32),
+        ],
+        compiler_params=pltpu.CompilerParams(vmem_limit_bytes=32 * 2**20),
+        cost_estimate=pl.CostEstimate(
+            flops=12 * count * P_SIZE**2, bytes_accessed=10 * 2**20, transcendentals=0
+        ),
+    )(place, *lefts, first_inverse, second_inverse, cross)
+
+
+def cols_kernel(chips, place, natural, *refs):
+    evens, odds = refs[:chips], refs[chips]
+    first_factor, first_inverse, second_factor, second_inverse, cross = refs[chips + 1 : chips + 6]
+    rounded, own, result = refs[chips + 6 : chips + 9]
+    given_cols, first_side, second_side, copied = refs[chips + 9 :]
+    row_index, column_index = place[0], place[1]
+    tile_rows = evens[0].shape[0] // 2
+    order, half = P_SIZE, P_SIZE // 2
+    step = pl.program_id(0)
+    width = 2 * BLOCK
+
+    def copies():
+        for chip in range(chips):
+            for core in range(2):
+                source = odds.at[chip] if core else evens[chip]
+                first = pl.multiple_of((row_index ^ (2 * chip + core)) * tile_rows, tile_rows)
+                for t in range(2):
+                    yield pltpu.make_async_copy(
+                        source.at[pl.ds(t * tile_rows, tile_rows), :],
+                        given_cols.at[pl.ds(t * order + first, tile_rows), :],
+                        copied.at[(2 * chip + core) * 2 + t],
+                    )
+
+    @pl.when(step == 0)
+    def _():
+        for copy in copies():
+            copy.start()
+        high, low = split(first_inverse[...])
+        first_side[:, 0:order] = high
+        first_side[:, order:] = low
+        high, low = split(second_inverse[...])
+        second_side[:, 0:order] = high
+        second_side[:, order : 2 * order] = high
+        second_side[:, 2 * order :] = low
+        own_row = pl.multiple_of(row_index * tile_rows, tile_rows)
+        own_col = pl.multiple_of(column_index * BLOCK, BLOCK)
+        tile = (pl.ds(own_row, tile_rows), pl.ds(own_col, BLOCK))
+        for t in range(NT):
+            rows = slice(t * tile_rows, (t + 1) * tile_rows)
+            result[t, 0] = first_factor[tile] if t == 0 else own[rows, 0:BLOCK]
+            if t == 0:
+                result[t, 1] = jnp.zeros((tile_rows, BLOCK), jnp.float32)
+            else:
+                result[t, 1] = second_factor[tile] if t == 1 else own[rows, BLOCK:]
+        for copy in copies():
+            copy.wait()
+
+    @pl.when(step > 0)
+    def _():
+        here = pl.ds(pl.multiple_of(step * width, width), width)
+
+        def lower_dot(side, parts):
+            upper_side = jnp.concatenate(
+                [side[0:half, k * order : k * order + half] for k in range(len(parts))], axis=1
+            )
+            upper = fast_dot(upper_side, jnp.concatenate([part[0:half] for part in parts]))
+            lower = fast_dot(side[half:order, :], jnp.concatenate(parts))
+            return jnp.concatenate([upper, lower])
+
+        given = given_cols[0:order, here]
+        first = lower_dot(first_side, [given, given]).astype(jnp.bfloat16)
+        left_over = given_cols[order:, here].astype(jnp.float32) - fast_dot(cross[...], first)
+        high, low = split(left_over)
+        second = lower_dot(second_side, [high, low, high]).astype(jnp.bfloat16)
+        begin = 2 * tile_rows
+        product = fast_dot(rounded[begin:, :], jnp.concatenate([first, second]))
+        kept = natural[begin:, :].astype(jnp.float32) - product
+        for s in range(2):
+            for t in range(NT):
+                if t < 2:
+                    result[t, s] = jnp.zeros((tile_rows, BLOCK), jnp.float32)
+                else:
+                    result[t, s] = kept[
+                        (t - 2) * tile_rows : (t - 1) * tile_rows, s * BLOCK : (s + 1) * BLOCK
+                    ]
+
+
+def solve_cols(place, natural, evens, odds, factors, rounded, own, tile_rows):
+    chips = len(evens)
+    square = whole((P_SIZE, P_SIZE))
+    return pl.pallas_call(
+        functools.partial(cols_kernel, chips),
+        grid=(NT // 2,),
+        in_specs=[
+            pl.BlockSpec(memory_space=pltpu.SMEM),
+            pl.BlockSpec((NT * tile_rows, 2 * BLOCK), lambda j: (0, j)),
+            *[pl.BlockSpec(memory_space=pl.ANY)] * (chips + 1),
             *[square] * 5,
-        ],
-        out_specs=pl.BlockSpec((group, NT, tile_rows, BLOCK), lambda i: (i, 0, 0, 0)),
+            whole(rounded.shape),
+            whole(own.shape),
+        ],
+        out_specs=pl.BlockSpec((NT, 2, tile_rows, BLOCK), lambda j: (0, j, 0, 0)),
         out_shape=jax.ShapeDtypeStruct((NT, NT, tile_rows, BLOCK), jnp.float32),
         scratch_shapes=[
             pltpu.VMEM((2 * P_SIZE, NT * BLOCK), jnp.bfloat16),
-            pltpu.VMEM((2 * P_SIZE, NT * BLOCK), jnp.bfloat16),
-            *[half] * 5,
-            pltpu.VMEM((rows, 2 * P_SIZE), jnp.float32),
-            pltpu.SemaphoreType.DMA((2 * len(tops),)),
-        ],
-        compiler_params=pltpu.CompilerParams(vmem_limit_bytes=56 * 2**20),
-    )(place, natural, *lefts, *tops, *factors)
+            pltpu.VMEM((P_SIZE, 2 * P_SIZE), jnp.bfloat16),
+            pltpu.VMEM((P_SIZE, 3 * P_SIZE), jnp.bfloat16),
+            pltpu.SemaphoreType.DMA((4 * chips,)),
+        ],
+        compiler_params=pltpu.CompilerParams(vmem_limit_bytes=48 * 2**20),
+        cost_estimate=pl.CostEstimate(
+            flops=10 * 10**9, bytes_accessed=24 * 2**20, transcendentals=0
+        ),
+    )(place, natural, *evens, odds, *factors, rounded, own)
 
 
 def swap(value, axis, offset):
     count = lax.axis_size(axis)
     return lax.ppermute(value, axis, [(i, i ^ offset) for i in range(count)])
+
+
+def double(value, axis, offsets):
+    value = value[None]
+    for offset in offsets:
+        value = jnp.concatenate([value, swap(value, axis, offset)])
+    return value
+
+
+def powers(begin, count):
+    offsets = []
+    while begin < count:
+        offsets.append(begin)
+        begin *= 2
+    return offsets
 
 
 def per_device(kernel):
@@ -467,20 +548,23 @@
     corner, top = take_top(tiles, tile_rows)
     natural, left = take_natural(tiles, tile_rows)
     chips = range(2, row_count, 2)
-    over_cols = jnp.stack([corner] + [swap(corner, "col", d) for d in range(1, col_count)])
-    near = jnp.stack([over_cols] + [swap(over_cols, "row", d) for d in chips])
+    over_cols = double(corner, "col", powers(1, col_count))
+    near = double(over_cols[:, 0:1], "row", powers(2, row_count))
     far = swap(near, "row", 1)
+    other = over_cols[:, 1:]
+    other_near = jnp.stack([other] + [swap(other, "row", d) for d in chips])
+    first_factor, first_inverse = factor_call(first_kernel, place, (near, far), (), [])
+    other_far = swap(other_near, "row", 1)
     lefts = [left] + [swap(left, "col", d) for d in range(1, col_count)]
-    even = [top] + [swap(top, "row", d) for d in chips]
-    first_factor, first_inverse = factor_call(first_kernel, place, (near, far), (), [])
-    odd = [swap(value, "row", 1) for value in even]
+    evens = [top] + [swap(top, "row", d) for d in chips]
     half = jax.ShapeDtypeStruct((P_SIZE, P_SIZE), jnp.bfloat16)
     second_factor, second_inverse, cross = factor_call(
-        second_kernel, place, (near, far), (first_inverse,), [half]
-    )
-    tops = [value for pair in zip(even, odd) for value in pair]
+        second_kernel, place, (other_near, other_far), (first_inverse,), [half]
+    )
+    odds = swap(jnp.stack(evens), "row", 1)
+    rounded, own = solve_rows(place, lefts, first_inverse, second_inverse, cross)
     factors = (first_factor, first_inverse, second_factor, second_inverse, cross)
-    result = tail(place, natural, lefts, tops, factors, tile_rows)
+    result = solve_cols(place, natural, evens, odds, factors, rounded, own, tile_rows)
     return result.reshape(kernel.shape)
 
 

time: 118 us -> 123 us (1.042)
  the two profiles are of different devices: /device:TPU:9 before, /device:TPU:1 now
where the time goes in v1:
time: 123 us
  Pallas kernels  64 us (52%)
  starting transfers between devices  25.8 us (21%)
  waiting for transfers between devices  22.1 us (18%)
  local copies, waits for them, and re-layouts  10.1 us (8%)
    pallas_call x2, Pallas kernels, factor_call(): pl.pallas_call(body, in_specs=[pl.BlockSpec(memory_space=pltpu.SMEM)] + [...  37.2 us
    ppermute x16, starting transfers between devices, swap(): return lax.ppermute(value, axis, [(i, i ^ offset) for i in range(count)])  25.8 us
    ppermute x16, waiting for transfers between devices, swap(): return lax.ppermute(value, axis, [(i, i ^ offset) for i in range(count)])  22.1 us
    pallas_call x1, Pallas kernels, solve_cols(): pl.pallas_call(functools.partial(cols_kernel, chips), grid=(NT // 2,), in...  17.2 us
    unnamed x14, local copies, waits for them, and re-layouts  10.1 us
    pallas_call x1, Pallas kernels, solve_rows(): pl.pallas_call(rows_kernel, grid=(count // rows,), in_specs=[pl.BlockSpec...  5.7 us
    pallas_call x1, Pallas kernels, take_natural(): pl.pallas_call(natural_kernel, grid=(NT,), in_specs=[pl.BlockSpec((1, NT,...  3.47 us
  transfers between devices with their start and end apart: 16, of which 4 were waited for; matrix products, arithmetic and copies ran while one was open for 0% of the time, Pallas kernels for 38%

profile of v1, /device:TPU:1, one launch (start us, length us, event | category | flops | bytes accessed | tf_op | source)
XLA Modules:
  0.0 122.8 jit_solution(4066379370800645101)
XLA Ops:
  0.0 2.2 %copy-done = bf16[16,1,16,1,8192]{4,2,3,1,0:T(8,128)(2,1)S(1)} copy-done((bf16[16,1,16,1,8192]{4,2,3,1,0:T(8,128)(2,1)S(1)}, bf16[16,1,16,1,8192]{4,2,3,1,0:T(8,128)(2,1)}, u32[]{:S(2)}) %copy-start) | copy-done | bytes 4194328
  2.6 2.2 %collective-permute-start.4 = (bf16[1,3,64,128]{3,2,1,0:T(8,128)(2,1)S(1)}, bf16[1,3,64,128]{3,2,1,0:T(8,128)(2,1)S(1)}, u32[]{:S(2)}, u32[]{:S(2)}) collective-permute-start(bf16[1,3,64,128]{3,2,1,0:T(8,128)(2,1)S(1)} %bitcast.21), channel_id=1, source_target_pairs={{0,1},{1,0},{2,3},{3,2},{4,5},{5,4},{6,7},{7,6},{8,9},{9,8},{10,11... | collective-permute-start | bytes 147464 | tf_op jit(solution)/shard_map/ppermute | solution.py:522
  4.8 1.5 %collective-permute-done.4 = bf16[1,3,64,128]{3,2,1,0:T(8,128)(2,1)S(1)} collective-permute-done((bf16[1,3,64,128]{3,2,1,0:T(8,128)(2,1)S(1)}, bf16[1,3,64,128]{3,2,1,0:T(8,128)(2,1)S(1)}, u32[]{:S(2)}, u32[]{:S(2)}) %collective-permute-start.4) | collective-permute-done | bytes 49184 | tf_op jit(solution)/shard_map/ppermute | solution.py:522
  6.3 2.5 %collective-permute-start.5 = (bf16[2,3,64,128]{3,2,1,0:T(8,128)(2,1)S(1)}, bf16[2,3,64,128]{3,2,1,0:T(8,128)(2,1)S(1)}, u32[]{:S(2)}, u32[]{:S(2)}) collective-permute-start(bf16[2,3,64,128]{3,2,1,0:T(8,128)(2,1)S(1)} %pad_maximum_fusion.6), channel_id=1, source_target_pairs={{0,2},{1,3},{2,0},{3,1},{4,6},{5,7},{6,4},{7,5},{8,10},{9,11},{10,... | collective-permute-start | bytes 294920 | tf_op jit(solution)/shard_map/ppermute | solution.py:522
  8.8 2.0 %collective-permute-done.5 = bf16[2,3,64,128]{3,2,1,0:T(8,128)(2,1)S(1)} collective-permute-done((bf16[2,3,64,128]{3,2,1,0:T(8,128)(2,1)S(1)}, bf16[2,3,64,128]{3,2,1,0:T(8,128)(2,1)S(1)}, u32[]{:S(2)}, u32[]{:S(2)}) %collective-permute-start.5) | collective-permute-done | bytes 98336 | tf_op jit(solution)/shard_map/ppermute | solution.py:522
  10.8 1.3 %collective-permute-start.6 = (bf16[1,4,1,64,128]{4,3,1,2,0:T(8,128)(2,1)S(1)}, bf16[1,4,1,64,128]{4,3,1,2,0:T(8,128)(2,1)S(1)}, u32[]{:S(2)}, u32[]{:S(2)}) collective-permute-start(bf16[1,4,1,64,128]{4,3,1,2,0:T(8,128)(2,1)S(1)} %maximum_bitcast_fusion), channel_id=1, source_target_pairs={{0,8},{4,12},{8,0},{12,4},{16,24},{20,28},{24,16},{28,20},{1,9},{5... | collective-permute-start | bytes 196616 | tf_op jit(solution)/shard_map/ppermute | solution.py:522
  12.5 2.2 %collective-permute-start.2 = (bf16[128,2048]{1,0:T(8,128)(2,1)S(1)}, bf16[128,2048]{1,0:T(8,128)(2,1)S(1)}, u32[]{:S(2)}, u32[]{:S(2)}) collective-permute-start(bf16[128,2048]{1,0:T(8,128)(2,1)S(1)} %get-tuple-element.17.refs_0_), channel_id=1, source_target_pairs={{0,24},{4,28},{8,16},{12,20},{16,8},{20,12},{24,0},{28,4},{1,25},{... | collective-permute-start | bytes 1572872 | tf_op jit(solution)/shard_map/ppermute | solution.py:522
  15.1 1.3 %collective-permute-start.10 = (bf16[4,2,64,128]{3,2,1,0:T(8,128)(2,1)S(1)}, bf16[4,2,64,128]{3,2,1,0:T(8,128)(2,1)S(1)}, u32[]{:S(2)}, u32[]{:S(2)}) collective-permute-start(bf16[4,2,64,128]{3,2,1,0:T(8,128)(2,1)S(1)} %pad_maximum_fusion.3), channel_id=1, source_target_pairs={{0,16},{4,20},{8,24},{12,28},{16,0},{20,4},{24,8},{28,12},{1,17},{... | collective-permute-start | bytes 393224 | tf_op jit(solution)/shard_map/ppermute | solution.py:522
  16.5 2.2 %copy-done.1 = bf16[16,1,16,1,8192]{4,2,3,1,0:T(8,128)(2,1)S(1)} copy-done((bf16[16,1,16,1,8192]{4,2,3,1,0:T(8,128)(2,1)S(1)}, bf16[16,1,16,1,8192]{4,2,3,1,0:T(8,128)(2,1)}, u32[]{:S(2)}) %copy-start.1) | copy-done | bytes 4194328
  18.7 3.5 %shard_map.17 = (bf16[1024,2048]{1,0:T(8,128)(2,1)S(1)}, bf16[1024,256]{1,0:T(8,128)(2,1)S(1)}) custom-call(bf16[16,16,8192]{2,1,0:T(8,128)(2,1)S(1)} %bitcast.20), custom_call_target="tpu_custom_call" | custom-call | bytes 33554432 | tf_op jit(solution)/shard_map/pallas_call | solution.py:275
  22.2 1.9 %copy-done.2 = bf16[1024,2048]{1,0:T(8,128)(2,1)} copy-done((bf16[1024,2048]{1,0:T(8,128)(2,1)}, bf16[1024,2048]{1,0:T(8,128)(2,1)S(1)}, u32[]{:S(2)}) %copy-start.2) | copy-done | bytes 4194328
  24.1 1.2 collective-permute-start.11
  25.3 17.0 %collective-permute-done.10 = bf16[4,2,64,128]{3,2,1,0:T(8,128)(2,1)S(1)} collective-permute-done((bf16[4,2,64,128]{3,2,1,0:T(8,128)(2,1)S(1)}, bf16[4,2,64,128]{3,2,1,0:T(8,128)(2,1)S(1)}, u32[]{:S(2)}, u32[]{:S(2)}) %collective-permute-start.10) | collective-permute-done | bytes 131104 | tf_op jit(solution)/shard_map/ppermute | solution.py:522
  42.5 4.3 %collective-permute-start.15 = (bf16[1024,256]{1,0:T(8,128)(2,1)S(1)}, bf16[1024,256]{1,0:T(8,128)(2,1)S(1)}, u32[]{:S(2)}, u32[]{:S(2)}) collective-permute-start(bf16[1024,256]{1,0:T(8,128)(2,1)S(1)} %get-tuple-element.24.refs_0_), channel_id=1, source_target_pairs={{0,3},{1,2},{2,1},{3,0},{4,7},{5,6},{6,5},{7,4},{8,11},{9,10},{10,... | collective-permute-start | bytes 1572872 | tf_op jit(solution)/shard_map/ppermute | solution.py:522
  46.9 2.0 %collective-permute-start.14 = (bf16[1024,256]{1,0:T(8,128)(2,1)S(1)}, bf16[1024,256]{1,0:T(8,128)(2,1)S(1)}, u32[]{:S(2)}, u32[]{:S(2)}) collective-permute-start(bf16[1024,256]{1,0:T(8,128)(2,1)S(1)} %get-tuple-element.24.refs_0_), channel_id=1, source_target_pairs={{0,2},{1,3},{2,0},{3,1},{4,6},{5,7},{6,4},{7,5},{8,10},{9,11},{10,... | collective-permute-start | bytes 1572872 | tf_op jit(solution)/shard_map/ppermute | solution.py:522
  49.0 2.2 %collective-permute-start.13 = (bf16[1024,256]{1,0:T(8,128)(2,1)S(1)}, bf16[1024,256]{1,0:T(8,128)(2,1)S(1)}, u32[]{:S(2)}, u32[]{:S(2)}) collective-permute-start(bf16[1024,256]{1,0:T(8,128)(2,1)S(1)} %get-tuple-element.24.refs_0_), channel_id=1, source_target_pairs={{0,1},{1,0},{2,3},{3,2},{4,5},{5,4},{6,7},{7,6},{8,9},{9,8},{10,11... | collective-permute-start | bytes 1572872 | tf_op jit(solution)/shard_map/ppermute | solution.py:522
  51.2 5.2 %collective-permute-start.12 = (bf16[4,4,2,64,128]{4,3,2,1,0:T(8,128)(2,1)S(1)}, bf16[4,4,2,64,128]{4,3,2,1,0:T(8,128)(2,1)S(1)}, u32[]{:S(2)}, u32[]{:S(2)}) collective-permute-start(bf16[4,4,2,64,128]{4,3,2,1,0:T(8,128)(2,1)S(1)} %pad_maximum_fusion.1.near), channel_id=1, source_target_pairs={{0,4},{4,0},{8,12},{12,8},{16,20},{20,16},{24,28},{28,24},{1,5},{5... | collective-permute-start | bytes 1572872 | tf_op jit(solution)/shard_map/ppermute | solution.py:522
  56.7 1.6 %collective-permute-done.8 = bf16[4,4,1,64,128]{4,3,1,2,0:T(8,128)(2,1)S(1)} collective-permute-done((bf16[4,4,1,64,128]{4,3,1,2,0:T(8,128)(2,1)S(1)}, bf16[4,4,1,64,128]{4,3,1,2,0:T(8,128)(2,1)S(1)}, u32[]{:S(2)}, u32[]{:S(2)}) %collective-permute-start.8) | collective-permute-done | bytes 262176 | tf_op jit(solution)/shard_map/ppermute | solution.py:522
  58.7 18.0 %shard_map.19 = (f32[512,512]{1,0:T(8,128)S(1)}, f32[512,512]{1,0:T(8,128)S(1)}) custom-call(s32[2]{0:T(128)S(1)} %pad_add_fusion.place, bf16[4,4,1,64,128]{4,3,2,1,0:T(8,128)(2,1)S(1)} %get-tuple-element.28.near, bf16[4,4,1,64,128]{4,3,2,1,0:T(8,128)(2,1)S(1)} %bitcast.30), custom_call_target="tpu_custom_call" | custom-call | flops 20000000000 | bytes 4194304 | tf_op jit(solution)/shard_map/pallas_call | solution.py:333
  76.7 19.2 %shard_map.20 = (f32[512,512]{1,0:T(8,128)S(1)}, f32[512,512]{1,0:T(8,128)S(1)}, bf16[512,512]{1,0:T(8,128)(2,1)S(1)}) custom-call(s32[2]{0:T(128)S(1)} %pad_add_fusion.place, bf16[4,4,2,64,128]{4,3,2,1,0:T(8,128)(2,1)S(1)} %pad_maximum_fusion.1.near, bf16[4,4,2,64,128]{4,3,2,1,0:T(8,128)(2,1)S(1)} %collective-permute-done.12.far, ...), custom_call_target="tpu_custom_call" | custom-call | flops 20000000000 | bytes 4194304 | tf_op jit(solution)/shard_map/pallas_call | solution.py:333
  95.9 5.7 %shard_map.21 = (bf16[1024,1024]{1,0:T(8,128)(2,1)S(1)}, f32[1024,256]{1,0:T(8,128)S(1)}) custom-call(s32[2]{0:T(128)S(1)} %pad_add_fusion.place, bf16[1024,256]{1,0:T(8,128)(2,1)S(1)} %get-tuple-element.24.refs_0_, bf16[1024,256]{1,0:T(8,128)(2,1)S(1)} %collective-permute-done.13.refs_1_, bf16[1024,256]{1,0:T(8,128)(2,1)S(1)} %collective-permute-done.14.refs_2_, ...), custom_call_target="tpu_custom_call" | custom-call | flops 3221225472 | bytes 10485760 | tf_op jit(solution)/shard_map/pallas_call | solution.py:385
  101.7 1.4 %copy-done.3 = bf16[1024,1024]{1,0:T(8,128)(2,1)} copy-done((bf16[1024,1024]{1,0:T(8,128)(2,1)}, bf16[1024,1024]{1,0:T(8,128)(2,1)S(1)}, u32[]{:S(2)}) %copy-start.3) | copy-done | bytes 2097176
  104.1 1.3 %copy-done.6 = bf16[4,128,2048]{2,1,0:T(8,128)(2,1)} copy-done((bf16[4,128,2048]{2,1,0:T(8,128)(2,1)}, bf16[4,128,2048]{2,1,0:T(8,128)(2,1)S(1)}, u32[]{:S(2)}) %copy-start.6) | copy-done | bytes 2097176
  105.4 17.2 %shard_map.22 = f32[16,16,64,128]{3,2,1,0:T(8,128)} custom-call(s32[2]{0:T(128)S(1)} %pad_add_fusion.place, bf16[1024,2048]{1,0:T(8,128)(2,1)} %copy-done.2, bf16[128,2048]{1,0:T(8,128)(2,1)S(1)} %get-tuple-element.17.refs_0_, bf16[128,2048]{1,0:T(8,128)(2,1)S(1)} %collective-permute-done.refs_1_, bf16[128,2048]{1,0:T(8,128)(2,1)S(1)} %collective-permute-done.1.refs_2_, ...), custom_call_target="tpu_custom_call" | custom-call | flops 10000000000 | bytes 25165824 | tf_op jit(solution)/shard_map/pallas_call | solution.py:494
  (37 shorter events, 3.3 us)
Async XLA Ops:
  0.0 2.2 %copy-start = (bf16[16,1,16,1,8192]{4,2,3,1,0:T(8,128)(2,1)S(1)}, bf16[16,1,16,1,8192]{4,2,3,1,0:T(8,128)(2,1)}, u32[]{:S(2)}) copy-start(bf16[16,1,16,1,8192]{4,2,3,1,0:T(8,128)(2,1)} %param.1) | copy-start | bytes 12582916
  2.6 3.7 %collective-permute-start.4 = (bf16[1,3,64,128]{3,2,1,0:T(8,128)(2,1)S(1)}, bf16[1,3,64,128]{3,2,1,0:T(8,128)(2,1)S(1)}, u32[]{:S(2)}, u32[]{:S(2)}) collective-permute-start(bf16[1,3,64,128]{3,2,1,0:T(8,128)(2,1)S(1)} %bitcast.21), channel_id=1, source_target_pairs={{0,1},{1,0},{2,3},{3,2},{4,5},{5,4},{6,7},{7,6},{8,9},{9,8},{10,11... | collective-permute-start | bytes 147464 | tf_op jit(solution)/shard_map/ppermute | solution.py:522
  6.3 4.5 %collective-permute-start.5 = (bf16[2,3,64,128]{3,2,1,0:T(8,128)(2,1)S(1)}, bf16[2,3,64,128]{3,2,1,0:T(8,128)(2,1)S(1)}, u32[]{:S(2)}, u32[]{:S(2)}) collective-permute-start(bf16[2,3,64,128]{3,2,1,0:T(8,128)(2,1)S(1)} %pad_maximum_fusion.6), channel_id=1, source_target_pairs={{0,2},{1,3},{2,0},{3,1},{4,6},{5,7},{6,4},{7,5},{8,10},{9,11},{10,... | collective-permute-start | bytes 294920 | tf_op jit(solution)/shard_map/ppermute | solution.py:522
  10.8 4.3 %collective-permute-start.6 = (bf16[1,4,1,64,128]{4,3,1,2,0:T(8,128)(2,1)S(1)}, bf16[1,4,1,64,128]{4,3,1,2,0:T(8,128)(2,1)S(1)}, u32[]{:S(2)}, u32[]{:S(2)}) collective-permute-start(bf16[1,4,1,64,128]{4,3,1,2,0:T(8,128)(2,1)S(1)} %maximum_bitcast_fusion), channel_id=1, source_target_pairs={{0,8},{4,12},{8,0},{12,4},{16,24},{20,28},{24,16},{28,20},{1,9},{5... | collective-permute-start | bytes 196616 | tf_op jit(solution)/shard_map/ppermute | solution.py:522
  12.2 11.9 %collective-permute-start.9 = (bf16[4,2,64,128]{3,2,1,0:T(8,128)(2,1)S(1)}, bf16[4,2,64,128]{3,2,1,0:T(8,128)(2,1)S(1)}, u32[]{:S(2)}, u32[]{:S(2)}) collective-permute-start(bf16[4,2,64,128]{3,2,1,0:T(8,128)(2,1)S(1)} %pad_maximum_fusion.3), channel_id=1, source_target_pairs={{0,8},{4,12},{8,0},{12,4},{16,24},{20,28},{24,16},{28,20},{1,9},{5... | collective-permute-start | bytes 393224 | tf_op jit(solution)/shard_map/ppermute | solution.py:522
  12.5 36.5 %collective-permute-start.2 = (bf16[128,2048]{1,0:T(8,128)(2,1)S(1)}, bf16[128,2048]{1,0:T(8,128)(2,1)S(1)}, u32[]{:S(2)}, u32[]{:S(2)}) collective-permute-start(bf16[128,2048]{1,0:T(8,128)(2,1)S(1)} %get-tuple-element.17.refs_0_), channel_id=1, source_target_pairs={{0,24},{4,28},{8,16},{12,20},{16,8},{20,12},{24,0},{28,4},{1,25},{... | collective-permute-start | bytes 1572872 | tf_op jit(solution)/shard_map/ppermute | solution.py:522
  14.7 36.5 %collective-permute-start.1 = (bf16[128,2048]{1,0:T(8,128)(2,1)S(1)}, bf16[128,2048]{1,0:T(8,128)(2,1)S(1)}, u32[]{:S(2)}, u32[]{:S(2)}) collective-permute-start(bf16[128,2048]{1,0:T(8,128)(2,1)S(1)} %get-tuple-element.17.refs_0_), channel_id=1, source_target_pairs={{0,16},{4,20},{8,24},{12,28},{16,0},{20,4},{24,8},{28,12},{1,17},{... | collective-permute-start | bytes 1572872 | tf_op jit(solution)/shard_map/ppermute | solution.py:522
  14.9 41.5 %collective-permute-start = (bf16[128,2048]{1,0:T(8,128)(2,1)S(1)}, bf16[128,2048]{1,0:T(8,128)(2,1)S(1)}, u32[]{:S(2)}, u32[]{:S(2)}) collective-permute-start(bf16[128,2048]{1,0:T(8,128)(2,1)S(1)} %get-tuple-element.17.refs_0_), channel_id=1, source_target_pairs={{0,8},{4,12},{8,0},{12,4},{16,24},{20,28},{24,16},{28,20},{1,9},{5... | collective-permute-start | bytes 1572872 | tf_op jit(solution)/shard_map/ppermute | solution.py:522
  15.1 27.2 %collective-permute-start.10 = (bf16[4,2,64,128]{3,2,1,0:T(8,128)(2,1)S(1)}, bf16[4,2,64,128]{3,2,1,0:T(8,128)(2,1)S(1)}, u32[]{:S(2)}, u32[]{:S(2)}) collective-permute-start(bf16[4,2,64,128]{3,2,1,0:T(8,128)(2,1)S(1)} %pad_maximum_fusion.3), channel_id=1, source_target_pairs={{0,16},{4,20},{8,24},{12,28},{16,0},{20,4},{24,8},{28,12},{1,17},{... | collective-permute-start | bytes 393224 | tf_op jit(solution)/shard_map/ppermute | solution.py:522
  16.5 2.2 %copy-start.1 = (bf16[16,1,16,1,8192]{4,2,3,1,0:T(8,128)(2,1)S(1)}, bf16[16,1,16,1,8192]{4,2,3,1,0:T(8,128)(2,1)}, u32[]{:S(2)}) copy-start(bf16[16,1,16,1,8192]{4,2,3,1,0:T(8,128)(2,1)} %param.1) | copy-start | bytes 12582916
  22.2 1.9 %copy-start.2 = (bf16[1024,2048]{1,0:T(8,128)(2,1)}, bf16[1024,2048]{1,0:T(8,128)(2,1)S(1)}, u32[]{:S(2)}) copy-start(bf16[1024,2048]{1,0:T(8,128)(2,1)S(1)} %get-tuple-element.16.natural) | copy-start | bytes 12582916
  24.1 18.4 %collective-permute-start.11 = (bf16[4,2,64,128]{3,2,1,0:T(8,128)(2,1)S(1)}, bf16[4,2,64,128]{3,2,1,0:T(8,128)(2,1)S(1)}, u32[]{:S(2)}, u32[]{:S(2)}) collective-permute-start(bf16[4,2,64,128]{3,2,1,0:T(8,128)(2,1)S(1)} %pad_maximum_fusion.3), channel_id=1, source_target_pairs={{0,24},{4,28},{8,16},{12,20},{16,8},{20,12},{24,0},{28,4},{1,25},{... | collective-permute-start | bytes 393224 | tf_op jit(solution)/shard_map/ppermute | solution.py:522
  42.3 4.6 %collective-permute-start.7 = (bf16[2,4,1,64,128]{4,3,1,2,0:T(8,128)(2,1)S(1)}, bf16[2,4,1,64,128]{4,3,1,2,0:T(8,128)(2,1)S(1)}, u32[]{:S(2)}, u32[]{:S(2)}) collective-permute-start(bf16[2,4,1,64,128]{4,3,1,2,0:T(8,128)(2,1)S(1)} %pad_maximum_fusion.5), channel_id=1, source_target_pairs={{0,16},{4,20},{8,24},{12,28},{16,0},{20,4},{24,8},{28,12},{1,17},{... | collective-permute-start | bytes 393224 | tf_op jit(solution)/shard_map/ppermute | solution.py:522
  42.5 53.4 %collective-permute-start.15 = (bf16[1024,256]{1,0:T(8,128)(2,1)S(1)}, bf16[1024,256]{1,0:T(8,128)(2,1)S(1)}, u32[]{:S(2)}, u32[]{:S(2)}) collective-permute-start(bf16[1024,256]{1,0:T(8,128)(2,1)S(1)} %get-tuple-element.24.refs_0_), channel_id=1, source_target_pairs={{0,3},{1,2},{2,1},{3,0},{4,7},{5,6},{6,5},{7,4},{8,11},{9,10},{10,... | collective-permute-start | bytes 1572872 | tf_op jit(solution)/shard_map/ppermute | solution.py:522
  46.9 49.0 %collective-permute-start.14 = (bf16[1024,256]{1,0:T(8,128)(2,1)S(1)}, bf16[1024,256]{1,0:T(8,128)(2,1)S(1)}, u32[]{:S(2)}, u32[]{:S(2)}) collective-permute-start(bf16[1024,256]{1,0:T(8,128)(2,1)S(1)} %get-tuple-element.24.refs_0_), channel_id=1, source_target_pairs={{0,2},{1,3},{2,0},{3,1},{4,6},{5,7},{6,4},{7,5},{8,10},{9,11},{10,... | collective-permute-start | bytes 1572872 | tf_op jit(solution)/shard_map/ppermute | solution.py:522
  49.0 46.9 %collective-permute-start.13 = (bf16[1024,256]{1,0:T(8,128)(2,1)S(1)}, bf16[1024,256]{1,0:T(8,128)(2,1)S(1)}, u32[]{:S(2)}, u32[]{:S(2)}) collective-permute-start(bf16[1024,256]{1,0:T(8,128)(2,1)S(1)} %get-tuple-element.24.refs_0_), channel_id=1, source_target_pairs={{0,1},{1,0},{2,3},{3,2},{4,5},{5,4},{6,7},{7,6},{8,9},{9,8},{10,11... | collective-permute-start | bytes 1572872 | tf_op jit(solution)/shard_map/ppermute | solution.py:522
  51.2 25.5 %collective-permute-start.12 = (bf16[4,4,2,64,128]{4,3,2,1,0:T(8,128)(2,1)S(1)}, bf16[4,4,2,64,128]{4,3,2,1,0:T(8,128)(2,1)S(1)}, u32[]{:S(2)}, u32[]{:S(2)}) collective-permute-start(bf16[4,4,2,64,128]{4,3,2,1,0:T(8,128)(2,1)S(1)} %pad_maximum_fusion.1.near), channel_id=1, source_target_pairs={{0,4},{4,0},{8,12},{12,8},{16,20},{20,16},{24,28},{28,24},{1,5},{5... | collective-permute-start | bytes 1572872 | tf_op jit(solution)/shard_map/ppermute | solution.py:522
  56.4 1.9 %collective-permute-start.8 = (bf16[4,4,1,64,128]{4,3,1,2,0:T(8,128)(2,1)S(1)}, bf16[4,4,1,64,128]{4,3,1,2,0:T(8,128)(2,1)S(1)}, u32[]{:S(2)}, u32[]{:S(2)}) collective-permute-start(bf16[4,4,1,64,128]{4,3,1,2,0:T(8,128)(2,1)S(1)} %get-tuple-element.27), channel_id=1, source_target_pairs={{0,4},{4,0},{8,12},{12,8},{16,20},{20,16},{24,28},{28,24},{1,5},{5... | collective-permute-start | bytes 786440 | tf_op jit(solution)/shard_map/ppermute | solution.py:522
  58.3 45.8 %collective-permute-start.3 = (bf16[4,128,2048]{2,1,0:T(8,128)(2,1)S(1)}, bf16[4,128,2048]{2,1,0:T(8,128)(2,1)S(1)}, u32[]{:S(2)}, u32[]{:S(2)}) collective-permute-start(bf16[4,128,2048]{2,1,0:T(8,128)(2,1)S(1)} %pad_maximum_fusion), channel_id=1, source_target_pairs={{0,4},{4,0},{8,12},{12,8},{16,20},{20,16},{24,28},{28,24},{1,5},{5... | collective-permute-start | bytes 6291464 | tf_op jit(solution)/shard_map/ppermute | solution.py:522
  95.9 5.8 %copy-start.4 = (f32[512,512]{1,0:T(8,128)}, f32[512,512]{1,0:T(8,128)S(1)}, u32[]{:S(2)}) copy-start(f32[512,512]{1,0:T(8,128)S(1)} %get-tuple-element.22.refs_5_.refs_8_) | copy-start | bytes 3145732
  101.6 1.4 %copy-start.3 = (bf16[1024,1024]{1,0:T(8,128)(2,1)}, bf16[1024,1024]{1,0:T(8,128)(2,1)S(1)}, u32[]{:S(2)}) copy-start(bf16[1024,1024]{1,0:T(8,128)(2,1)S(1)} %get-tuple-element.25.refs_10_) | copy-start | bytes 6291460
  103.0 1.0 copy-start.5
  104.1 1.4 %copy-start.6 = (bf16[4,128,2048]{2,1,0:T(8,128)(2,1)}, bf16[4,128,2048]{2,1,0:T(8,128)(2,1)S(1)}, u32[]{:S(2)}) copy-start(bf16[4,128,2048]{2,1,0:T(8,128)(2,1)S(1)} %collective-permute-done.3.refs_4_) | copy-start | bytes 6291460

commit v2 on v1

--- a/solution.py
+++ b/solution.py
@@ -137,7 +137,7 @@
         factor_kernel,
         out_shape=[square, square],
         scratch_shapes=factor_scratch(),
-        compiler_params=pltpu.CompilerParams(vmem_limit_bytes=32 * 2**20),
+        compiler_params=pltpu.CompilerParams(vmem_limit_bytes=20 * 2**20),
     )(corner)
 
 
@@ -235,14 +235,20 @@
         )
 
 
-def top_kernel(tiles, corner, top, spread_rows):
+def top_kernel(tiles, corner, top, held, spread_rows, copied):
     tile_rows = corner.shape[1]
+    copies = [pltpu.make_async_copy(tiles.at[t], held.at[t], copied.at[t]) for t in range(2)]
+    for copy in copies:
+        copy.start()
     for t in range(2):
-        natural_tile(tiles[t], spread_rows, tile_rows)
+        copies[t].wait()
+        natural_tile(held[t], spread_rows, tile_rows)
         for s in range(NT):
             tile = spread_rows[pl.ds(s, tile_rows, stride=NT), :].astype(jnp.bfloat16)
-            top[t * tile_rows : (t + 1) * tile_rows, s * BLOCK : (s + 1) * BLOCK] = tile
-            if s <= t:
+            if s >= 2:
+                here = slice((s - 2) * BLOCK, (s - 1) * BLOCK)
+                top[t * tile_rows : (t + 1) * tile_rows, here] = tile
+            elif s <= t:
                 corner[t + s] = tile
 
 
@@ -259,15 +265,17 @@
 def take_top(tiles, tile_rows):
     return pl.pallas_call(
         top_kernel,
-        grid=(1,),
-        in_specs=[pl.BlockSpec((2, NT, tile_rows * BLOCK), lambda i: (0, 0, 0))],
-        out_specs=[whole((3, tile_rows, BLOCK)), whole((2 * tile_rows, NT * BLOCK))],
+        in_specs=[pl.BlockSpec(memory_space=pltpu.HBM)],
         out_shape=[
             jax.ShapeDtypeStruct((3, tile_rows, BLOCK), jnp.bfloat16),
-            jax.ShapeDtypeStruct((2 * tile_rows, NT * BLOCK), jnp.bfloat16),
-        ],
-        scratch_shapes=[pltpu.VMEM((tile_rows * NT, BLOCK), jnp.float32)],
-        compiler_params=pltpu.CompilerParams(vmem_limit_bytes=16 * 2**20),
+            jax.ShapeDtypeStruct((2 * tile_rows, (NT - 2) * BLOCK), jnp.bfloat16),
+        ],
+        scratch_shapes=[
+            pltpu.VMEM((2, NT, tile_rows * BLOCK), jnp.bfloat16),
+            pltpu.VMEM((tile_rows * NT, BLOCK), jnp.float32),
+            pltpu.SemaphoreType.DMA((2,)),
+        ],
+        compiler_params=pltpu.CompilerParams(vmem_limit_bytes=60 * 2**20),
     )(tiles)
 
 
@@ -278,14 +286,14 @@
         in_specs=[pl.BlockSpec((1, NT, tile_rows * BLOCK), lambda t: (t, 0, 0))],
         out_specs=[
             pl.BlockSpec((tile_rows, NT * BLOCK), lambda t: (t, 0)),
-            pl.BlockSpec((tile_rows, 2 * BLOCK), lambda t: (t, 0)),
+            pl.BlockSpec((tile_rows, 2 * BLOCK), lambda t: (jnp.maximum(t - 2, 0), 0)),
         ],
         out_shape=[
             jax.ShapeDtypeStruct((NT * tile_rows, NT * BLOCK), jnp.bfloat16),
-            jax.ShapeDtypeStruct((NT * tile_rows, 2 * BLOCK), jnp.bfloat16),
+            jax.ShapeDtypeStruct(((NT - 2) * tile_rows, 2 * BLOCK), jnp.bfloat16),
         ],
         scratch_shapes=[pltpu.VMEM((tile_rows * NT, BLOCK), jnp.float32)],
-        compiler_params=pltpu.CompilerParams(vmem_limit_bytes=16 * 2**20),
+        compiler_params=pltpu.CompilerParams(vmem_limit_bytes=60 * 2**20),
         cost_estimate=pl.CostEstimate(
             flops=0, bytes_accessed=16 * NT * tile_rows * NT * BLOCK, transcendentals=0
         ),
@@ -311,7 +319,7 @@
 
 
 def second_kernel(
-    place, near, far, first_inverse, factor, inverse, cross, rest, work, done
+    place, near, far, first_inverse, factor, inverse, cross, own, rest, work, done
 ):
     place_corner(place, (near, far), 0, rest)
     given = rest[...].astype(jnp.bfloat16)
@@ -320,14 +328,21 @@
         jnp.concatenate([given, given], axis=1),
         jnp.concatenate([high, low], axis=1),
         ((1,), (1,)),
-    ).astype(jnp.bfloat16)
+    )
+    rest[...] = solved
+    tile_rows, tile_cols = own.shape
+    own[...] = rest[
+        pl.ds(pl.multiple_of(place[0] * tile_rows, tile_rows), tile_rows),
+        pl.ds(pl.multiple_of(place[1] * tile_cols, tile_cols), tile_cols),
+    ]
+    solved = solved.astype(jnp.bfloat16)
     cross[...] = solved
     place_corner(place, (near, far), 1, rest)
     rest[...] = rest[...] - fast_dot(solved, solved, ((1,), (1,)))
     factor_rest(rest, factor, inverse, work, done)
 
 
-def factor_call(body, place, slots, extra, extra_out):
+def factor_call(body, place, slots, extra, extra_out, cost):
     square = jax.ShapeDtypeStruct((P_SIZE, P_SIZE), jnp.float32)
     on_vmem = pl.BlockSpec(memory_space=pltpu.VMEM)
     return pl.pallas_call(
@@ -335,9 +350,9 @@
         in_specs=[pl.BlockSpec(memory_space=pltpu.SMEM)] + [on_vmem] * (2 + len(extra)),
         out_shape=[square, square] + extra_out,
         scratch_shapes=factor_scratch(),
-        compiler_params=pltpu.CompilerParams(vmem_limit_bytes=32 * 2**20),
+        compiler_params=pltpu.CompilerParams(vmem_limit_bytes=20 * 2**20),
         cost_estimate=pl.CostEstimate(
-            flops=20 * 10**9, bytes_accessed=4 * 2**20, transcendentals=0
+            flops=cost, bytes_accessed=4 * 2**20, transcendentals=0
         ),
     )(place, *slots, *extra)
 
@@ -404,7 +419,7 @@
             pltpu.VMEM((3 * P_SIZE, P_SIZE), jnp.bfloat16),
             pltpu.VMEM((rows, 2 * P_SIZE), jnp.float32),
         ],
-        compiler_params=pltpu.CompilerParams(vmem_limit_bytes=32 * 2**20),
+        compiler_params=pltpu.CompilerParams(vmem_limit_bytes=24 * 2**20),
         cost_estimate=pl.CostEstimate(
             flops=12 * count * P_SIZE**2, bytes_accessed=10 * 2**20, transcendentals=0
         ),
@@ -414,8 +429,8 @@
 def cols_kernel(chips, place, natural, *refs):
     evens, odds = refs[:chips], refs[chips]
     first_factor, first_inverse, second_factor, second_inverse, cross = refs[chips + 1 : chips + 6]
-    rounded, own, result = refs[chips + 6 : chips + 9]
-    given_cols, first_side, second_side, copied = refs[chips + 9 :]
+    rounded, own, own_cross, result = refs[chips + 6 : chips + 10]
+    given_cols, first_side, second_side, copied = refs[chips + 10 :]
     row_index, column_index = place[0], place[1]
     tile_rows = evens[0].shape[0] // 2
     order, half = P_SIZE, P_SIZE // 2
@@ -448,19 +463,20 @@
         own_row = pl.multiple_of(row_index * tile_rows, tile_rows)
         own_col = pl.multiple_of(column_index * BLOCK, BLOCK)
         tile = (pl.ds(own_row, tile_rows), pl.ds(own_col, BLOCK))
-        for t in range(NT):
-            rows = slice(t * tile_rows, (t + 1) * tile_rows)
-            result[t, 0] = first_factor[tile] if t == 0 else own[rows, 0:BLOCK]
-            if t == 0:
-                result[t, 1] = jnp.zeros((tile_rows, BLOCK), jnp.float32)
-            else:
-                result[t, 1] = second_factor[tile] if t == 1 else own[rows, BLOCK:]
+        result[0, 0] = first_factor[tile]
+        result[0, 1] = jnp.zeros((tile_rows, BLOCK), jnp.float32)
+        result[1, 0] = own_cross[...]
+        result[1, 1] = second_factor[tile]
+        for t in range(2, NT):
+            rows = slice((t - 2) * tile_rows, (t - 1) * tile_rows)
+            result[t, 0] = own[rows, 0:BLOCK]
+            result[t, 1] = own[rows, BLOCK:]
         for copy in copies():
             copy.wait()
 
     @pl.when(step > 0)
     def _():
-        here = pl.ds(pl.multiple_of(step * width, width), width)
+        here = pl.ds(pl.multiple_of((step - 1) * width, width), width)
 
         def lower_dot(side, parts):
             upper_side = jnp.concatenate(
@@ -476,7 +492,7 @@
         high, low = split(left_over)
         second = lower_dot(second_side, [high, low, high]).astype(jnp.bfloat16)
         begin = 2 * tile_rows
-        product = fast_dot(rounded[begin:, :], jnp.concatenate([first, second]))
+        product = fast_dot(rounded[...], jnp.concatenate([first, second]))
         kept = natural[begin:, :].astype(jnp.float32) - product
         for s in range(2):
             for t in range(NT):
@@ -488,7 +504,7 @@
                     ]
 
 
-def solve_cols(place, natural, evens, odds, factors, rounded, own, tile_rows):
+def solve_cols(place, natural, evens, odds, factors, rounded, own, own_cross, tile_rows):
     chips = len(evens)
     square = whole((P_SIZE, P_SIZE))
     return pl.pallas_call(
@@ -501,20 +517,21 @@
             *[square] * 5,
             whole(rounded.shape),
             whole(own.shape),
+            whole(own_cross.shape),
         ],
         out_specs=pl.BlockSpec((NT, 2, tile_rows, BLOCK), lambda j: (0, j, 0, 0)),
         out_shape=jax.ShapeDtypeStruct((NT, NT, tile_rows, BLOCK), jnp.float32),
         scratch_shapes=[
-            pltpu.VMEM((2 * P_SIZE, NT * BLOCK), jnp.bfloat16),
+            pltpu.VMEM((2 * P_SIZE, (NT - 2) * BLOCK), jnp.bfloat16),
             pltpu.VMEM((P_SIZE, 2 * P_SIZE), jnp.bfloat16),
             pltpu.VMEM((P_SIZE, 3 * P_SIZE), jnp.bfloat16),
             pltpu.SemaphoreType.DMA((4 * chips,)),
         ],
-        compiler_params=pltpu.CompilerParams(vmem_limit_bytes=48 * 2**20),
+        compiler_params=pltpu.CompilerParams(vmem_limit_bytes=40 * 2**20),
         cost_estimate=pl.CostEstimate(
             flops=10 * 10**9, bytes_accessed=24 * 2**20, transcendentals=0
         ),
-    )(place, natural, *evens, odds, *factors, rounded, own)
+    )(place, natural, *evens, odds, *factors, rounded, own, own_cross)
 
 
 def swap(value, axis, offset):
@@ -551,20 +568,41 @@
     over_cols = double(corner, "col", powers(1, col_count))
     near = double(over_cols[:, 0:1], "row", powers(2, row_count))
     far = swap(near, "row", 1)
-    other = over_cols[:, 1:]
-    other_near = jnp.stack([other] + [swap(other, "row", d) for d in chips])
-    first_factor, first_inverse = factor_call(first_kernel, place, (near, far), (), [])
+    other, left, near, far = lax.optimization_barrier((over_cols[:, 1:], left, near, far))
+    other_near = [other] + [swap(other, "row", d) for d in chips]
+    lefts = {0: left}
+    for d in range(1, col_count):
+        if d != 2:
+            lefts[d] = swap(left, "col", d)
+    first_factor, first_inverse = factor_call(
+        first_kernel, place, (near, far), (), [], 40 * 10**9
+    )
+    others = [lefts[d] for d in sorted(lefts) if d]
+    *other_near, top, left, first_inverse = lax.optimization_barrier(
+        (*other_near, top, left, first_inverse, *others)
+    )[: len(other_near) + 3]
+    other_near = jnp.stack(other_near)
     other_far = swap(other_near, "row", 1)
-    lefts = [left] + [swap(left, "col", d) for d in range(1, col_count)]
+    if col_count > 2:
+        lefts[2] = swap(left, "col", 2)
+    lefts = [lefts[d] for d in range(col_count)]
     evens = [top] + [swap(top, "row", d) for d in chips]
-    half = jax.ShapeDtypeStruct((P_SIZE, P_SIZE), jnp.bfloat16)
-    second_factor, second_inverse, cross = factor_call(
-        second_kernel, place, (other_near, other_far), (first_inverse,), [half]
+    extra = [
+        jax.ShapeDtypeStruct((P_SIZE, P_SIZE), jnp.bfloat16),
+        jax.ShapeDtypeStruct((tile_rows, BLOCK), jnp.float32),
+    ]
+    second_factor, second_inverse, cross, own_cross = factor_call(
+        second_kernel, place, (other_near, other_far), (first_inverse,), extra, 40 * 10**9
+    )
+    *evens, second_inverse, lefts[2 % col_count] = lax.optimization_barrier(
+        (*evens, second_inverse, lefts[2 % col_count])
     )
     odds = swap(jnp.stack(evens), "row", 1)
     rounded, own = solve_rows(place, lefts, first_inverse, second_inverse, cross)
     factors = (first_factor, first_inverse, second_factor, second_inverse, cross)
-    result = solve_cols(place, natural, evens, odds, factors, rounded, own, tile_rows)
+    result = solve_cols(
+        place, natural, evens, odds, factors, rounded, own, own_cross, tile_rows
+    )
     return result.reshape(kernel.shape)
 
 

time: 123 us -> 117 us (0.951)
  Pallas kernels: 64 us -> 75.5 us
  local copies, waits for them, and re-layouts: 10.1 us -> 0.02 us
  waiting for transfers between devices: 22.1 us -> 13.6 us
  other arithmetic: 0.51 us -> 1.97 us
    unnamed x14 -> x6, local copies, waits for them, and re-layouts: 10.1 us -> 0.01 us
    ppermute x16, waiting for transfers between devices: 22.1 us -> 13.6 us  [swap(): return lax.ppermute(value, axis, [(i, i ^ offset) for i in range(count)])]
    pallas_call x1, Pallas kernels: 3.47 us -> 11.5 us  [take_natural(): pl.pallas_call(natural_kernel, grid=(NT,), in_specs=[pl.BlockSpec((1, NT,...]
    pallas_call x1, Pallas kernels: 17.2 us -> 19.5 us  [solve_cols(): pl.pallas_call(functools.partial(cols_kernel, chips), grid=(NT // 2,), in...]
    pallas_call x1, Pallas kernels: 0.4 us -> 2.14 us  [take_top(): pl.pallas_call(top_kernel, in_specs=[pl.BlockSpec(memory_space=pltpu.HBM)...]
  transfers between devices with their start and end apart: 16 -> 16, of which waited for: 4 -> 6; matrix products, arithmetic and copies ran while one was open for 0% -> 0% of each run, Pallas kernels for 38% -> 46%
where the time goes in v2:
time: 117 us; the launch traced here: 116 us
  Pallas kernels  75.5 us (65%)
  starting transfers between devices  25 us (21%)
  waiting for transfers between devices  13.6 us (12%)
  other arithmetic  1.97 us (2%)
    pallas_call x2, Pallas kernels, factor_call(): pl.pallas_call(body, in_specs=[pl.BlockSpec(memory_space=pltpu.SMEM)] + [...  37.3 us
    ppermute x16, starting transfers between devices, swap(): return lax.ppermute(value, axis, [(i, i ^ offset) for i in range(count)])  25 us
    pallas_call x1, Pallas kernels, solve_cols(): pl.pallas_call(functools.partial(cols_kernel, chips), grid=(NT // 2,), in...  19.5 us
    ppermute x16, waiting for transfers between devices, swap(): return lax.ppermute(value, axis, [(i, i ^ offset) for i in range(count)])  13.6 us
    pallas_call x1, Pallas kernels, take_natural(): pl.pallas_call(natural_kernel, grid=(NT,), in_specs=[pl.BlockSpec((1, NT,...  11.5 us
    pallas_call x1, Pallas kernels, solve_rows(): pl.pallas_call(rows_kernel, grid=(count // rows,), in_specs=[pl.BlockSpec...  5.05 us
  transfers between devices with their start and end apart: 16, of which 6 were waited for; matrix products, arithmetic and copies ran while one was open for 0% of the time, Pallas kernels for 46%

profile of v2, /device:TPU:1, one launch (start us, length us, event | category | flops | bytes accessed | tf_op | source)
XLA Modules:
  0.0 116.3 jit_solution(15179730629619560123)
XLA Ops:
  0.0 2.1 %shard_map.18 = (bf16[3,64,128]{2,1,0:T(8,128)(2,1)}, bf16[128,1792]{1,0:T(8,128)(2,1)}) custom-call(bf16[16,16,8192]{2,1,0:T(8,128)(2,1)} %bitcast.23), custom_call_target="tpu_custom_call" | custom-call | tf_op jit(solution)/shard_map/pallas_call | solution.py:266
  2.2 2.2 %collective-permute-start = (bf16[1,3,64,128]{3,2,1,0:T(8,128)(2,1)}, bf16[1,3,64,128]{3,2,1,0:T(8,128)(2,1)S(1)}, u32[]{:S(2)}, u32[]{:S(2)}) collective-permute-start(bf16[1,3,64,128]{3,2,1,0:T(8,128)(2,1)} %bitcast.26), channel_id=1, source_target_pairs={{0,1},{1,0},{2,3},{3,2},{4,5},{5,4},{6,7},{7,6},{8,9},{9,8},{10,11... | collective-permute-start | bytes 147464 | tf_op jit(solution)/shard_map/ppermute | solution.py:539
  4.3 1.7 %collective-permute-done = bf16[1,3,64,128]{3,2,1,0:T(8,128)(2,1)S(1)} collective-permute-done((bf16[1,3,64,128]{3,2,1,0:T(8,128)(2,1)}, bf16[1,3,64,128]{3,2,1,0:T(8,128)(2,1)S(1)}, u32[]{:S(2)}, u32[]{:S(2)}) %collective-permute-start) | collective-permute-done | bytes 49184 | tf_op jit(solution)/shard_map/ppermute | solution.py:539
  6.0 0.8 pad_maximum_fusion.5
  6.8 2.5 %collective-permute-start.1 = (bf16[2,3,64,128]{3,2,1,0:T(8,128)(2,1)S(1)}, bf16[2,3,64,128]{3,2,1,0:T(8,128)(2,1)S(1)}, u32[]{:S(2)}, u32[]{:S(2)}) collective-permute-start(bf16[2,3,64,128]{3,2,1,0:T(8,128)(2,1)S(1)} %pad_maximum_fusion.5), channel_id=1, source_target_pairs={{0,2},{1,3},{2,0},{3,1},{4,6},{5,7},{6,4},{7,5},{8,10},{9,11},{10,... | collective-permute-start | bytes 294920 | tf_op jit(solution)/shard_map/ppermute | solution.py:539
  9.4 2.0 %collective-permute-done.1 = bf16[2,3,64,128]{3,2,1,0:T(8,128)(2,1)S(1)} collective-permute-done((bf16[2,3,64,128]{3,2,1,0:T(8,128)(2,1)S(1)}, bf16[2,3,64,128]{3,2,1,0:T(8,128)(2,1)S(1)}, u32[]{:S(2)}, u32[]{:S(2)}) %collective-permute-start.1) | collective-permute-done | bytes 98336 | tf_op jit(solution)/shard_map/ppermute | solution.py:539
  11.4 0.7 maximum_bitcast_fusion
  12.1 1.3 %collective-permute-start.2 = (bf16[1,4,1,64,128]{4,3,1,2,0:T(8,128)(2,1)S(1)}, bf16[1,4,1,64,128]{4,3,1,2,0:T(8,128)(2,1)S(1)}, u32[]{:S(2)}, u32[]{:S(2)}) collective-permute-start(bf16[1,4,1,64,128]{4,3,1,2,0:T(8,128)(2,1)S(1)} %maximum_bitcast_fusion), channel_id=1, source_target_pairs={{0,8},{4,12},{8,0},{12,4},{16,24},{20,28},{24,16},{28,20},{1,9},{5... | collective-permute-start | bytes 196616 | tf_op jit(solution)/shard_map/ppermute | solution.py:539
  13.4 1.8 %collective-permute-done.2 = bf16[1,4,1,64,128]{4,3,1,2,0:T(8,128)(2,1)S(1)} collective-permute-done((bf16[1,4,1,64,128]{4,3,1,2,0:T(8,128)(2,1)S(1)}, bf16[1,4,1,64,128]{4,3,1,2,0:T(8,128)(2,1)S(1)}, u32[]{:S(2)}, u32[]{:S(2)}) %collective-permute-start.2) | collective-permute-done | bytes 65568 | tf_op jit(solution)/shard_map/ppermute | solution.py:539
  15.3 1.4 %collective-permute-start.3 = (bf16[2,4,1,64,128]{4,3,1,2,0:T(8,128)(2,1)S(1)}, bf16[2,4,1,64,128]{4,3,1,2,0:T(8,128)(2,1)S(1)}, u32[]{:S(2)}, u32[]{:S(2)}) collective-permute-start(bf16[2,4,1,64,128]{4,3,1,2,0:T(8,128)(2,1)S(1)} %pad_maximum_fusion.4), channel_id=1, source_target_pairs={{0,16},{4,20},{8,24},{12,28},{16,0},{20,4},{24,8},{28,12},{1,17},{... | collective-permute-start | bytes 393224 | tf_op jit(solution)/shard_map/ppermute | solution.py:539
  16.6 2.5 %collective-permute-done.3 = bf16[2,4,1,64,128]{4,3,1,2,0:T(8,128)(2,1)S(1)} collective-permute-done((bf16[2,4,1,64,128]{4,3,1,2,0:T(8,128)(2,1)S(1)}, bf16[2,4,1,64,128]{4,3,1,2,0:T(8,128)(2,1)S(1)}, u32[]{:S(2)}, u32[]{:S(2)}) %collective-permute-start.3) | collective-permute-done | bytes 131104 | tf_op jit(solution)/shard_map/ppermute | solution.py:539
  19.2 5.2 %collective-permute-start.4 = (bf16[4,4,1,64,128]{4,3,1,2,0:T(8,128)(2,1)S(1)}, bf16[4,4,1,64,128]{4,3,1,2,0:T(8,128)(2,1)S(1)}, u32[]{:S(2)}, u32[]{:S(2)}) collective-permute-start(bf16[4,4,1,64,128]{4,3,1,2,0:T(8,128)(2,1)S(1)} %pad_maximum_fusion.2), channel_id=1, source_target_pairs={{0,4},{4,0},{8,12},{12,8},{16,20},{20,16},{24,28},{28,24},{1,5},{5... | collective-permute-start | bytes 786440 | tf_op jit(solution)/shard_map/ppermute | solution.py:539
  24.3 11.5 %shard_map.17 = (bf16[1024,2048]{1,0:T(8,128)(2,1)}, bf16[896,256]{1,0:T(8,128)(2,1)}) custom-call(bf16[16,16,8192]{2,1,0:T(8,128)(2,1)} %bitcast.24), custom_call_target="tpu_custom_call" | custom-call | bytes 33554432 | tf_op jit(solution)/shard_map/pallas_call | solution.py:283
  36.0 2.5 %collective-permute-start.7 = (bf16[4,2,64,128]{3,2,1,0:T(8,128)(2,1)S(1)}, bf16[4,2,64,128]{3,2,1,0:T(8,128)(2,1)S(1)}, u32[]{:S(2)}, u32[]{:S(2)}) collective-permute-start(bf16[4,2,64,128]{3,2,1,0:T(8,128)(2,1)S(1)} %slice.8), channel_id=1, source_target_pairs={{0,24},{4,28},{8,16},{12,20},{16,8},{20,12},{24,0},{28,4},{1,25},{... | collective-permute-start | bytes 393224 | tf_op jit(solution)/shard_map/ppermute | solution.py:539
  38.8 4.4 %collective-permute-start.9 = (bf16[896,256]{1,0:T(8,128)(2,1)}, bf16[896,256]{1,0:T(8,128)(2,1)S(1)}, u32[]{:S(2)}, u32[]{:S(2)}) collective-permute-start(bf16[896,256]{1,0:T(8,128)(2,1)} %get-tuple-element.50.refs_0_), channel_id=1, source_target_pairs={{0,3},{1,2},{2,1},{3,0},{4,7},{5,6},{6,5},{7,4},{8,11},{9,10},{10,... | collective-permute-start | bytes 1376264 | tf_op jit(solution)/shard_map/ppermute | solution.py:539
  43.2 18.0 %shard_map.19 = (f32[512,512]{1,0:T(8,128)S(1)}, f32[512,512]{1,0:T(8,128)S(1)}) custom-call(s32[2]{0:T(128)S(1)} %pad_add_fusion.place, bf16[4,4,1,64,128]{4,3,2,1,0:T(8,128)(2,1)S(1)} %bitcast.21, bf16[4,4,1,64,128]{4,3,2,1,0:T(8,128)(2,1)S(1)} %bitcast.22), custom_call_target="tpu_custom_call" | custom-call | flops 40000000000 | bytes 4194304 | tf_op jit(solution)/shard_map/pallas_call | solution.py:348
  61.2 3.1 %collective-permute-done.8.refs_1_ = bf16[896,256]{1,0:T(8,128)(2,1)S(1)} collective-permute-done((bf16[896,256]{1,0:T(8,128)(2,1)}, bf16[896,256]{1,0:T(8,128)(2,1)S(1)}, u32[]{:S(2)}, u32[]{:S(2)}) %collective-permute-start.8) | collective-permute-done | bytes 458784 | tf_op jit(solution)/shard_map/ppermute | solution.py:539
  64.4 0.6 collective-permute-start.13
  64.9 2.2 %collective-permute-start.12 = (bf16[128,1792]{1,0:T(8,128)(2,1)S(1)}, bf16[128,1792]{1,0:T(8,128)(2,1)S(1)}, u32[]{:S(2)}, u32[]{:S(2)}) collective-permute-start(bf16[128,1792]{1,0:T(8,128)(2,1)S(1)} %copy-done), channel_id=1, source_target_pairs={{0,24},{4,28},{8,16},{12,20},{16,8},{20,12},{24,0},{28,4},{1,25},{... | collective-permute-start | bytes 1376264 | tf_op jit(solution)/shard_map/ppermute | solution.py:539
  67.9 19.3 %shard_map.20 = (f32[512,512]{1,0:T(8,128)S(1)}, f32[512,512]{1,0:T(8,128)S(1)}, bf16[512,512]{1,0:T(8,128)(2,1)S(1)}, f32[64,128]{1,0:T(8,128)S(1)}) custom-call(s32[2]{0:T(128)S(1)} %pad_add_fusion.place, bf16[4,4,2,64,128]{4,3,2,1,0:T(8,128)(2,1)S(1)} %pad_maximum_fusion.1.near, bf16[4,4,2,64,128]{4,3,2,1,0:T(8,128)(2,1)S(1)} %collective-permute-done.13.far, ...), custom_call_target="tpu_custom_call" | custom-call | flops 40000000000 | bytes 4194304 | tf_op jit(solution)/shard_map/pallas_call | solution.py:348
  87.2 2.4 %collective-permute-done.14.refs_2_ = bf16[896,256]{1,0:T(8,128)(2,1)S(1)} collective-permute-done((bf16[896,256]{1,0:T(8,128)(2,1)S(1)}, bf16[896,256]{1,0:T(8,128)(2,1)S(1)}, u32[]{:S(2)}, u32[]{:S(2)}) %collective-permute-start.14) | collective-permute-done | bytes 458784 | tf_op jit(solution)/shard_map/ppermute | solution.py:539
  89.9 1.7 %collective-permute-start.15 = (bf16[4,128,1792]{2,1,0:T(8,128)(2,1)S(1)}, bf16[4,128,1792]{2,1,0:T(8,128)(2,1)S(1)}, u32[]{:S(2)}, u32[]{:S(2)}) collective-permute-start(bf16[4,128,1792]{2,1,0:T(8,128)(2,1)S(1)} %pad_maximum_fusion), channel_id=1, source_target_pairs={{0,4},{4,0},{8,12},{12,8},{16,20},{20,16},{24,28},{28,24},{1,5},{5... | collective-permute-start | bytes 5505032 | tf_op jit(solution)/shard_map/ppermute | solution.py:539
  91.6 5.0 %shard_map.21 = (bf16[896,1024]{1,0:T(8,128)(2,1)S(1)}, f32[896,256]{1,0:T(8,128)S(1)}) custom-call(s32[2]{0:T(128)S(1)} %pad_add_fusion.place, bf16[896,256]{1,0:T(8,128)(2,1)S(1)} %copy-done.1, bf16[896,256]{1,0:T(8,128)(2,1)S(1)} %collective-permute-done.8.refs_1_, bf16[896,256]{1,0:T(8,128)(2,1)S(1)} %collective-permute-done.14.refs_2_, ...), custom_call_target="tpu_custom_call" | custom-call | flops 2818572288 | bytes 10485760 | tf_op jit(solution)/shard_map/pallas_call | solution.py:400
  96.7 19.5 %shard_map.22 = f32[16,16,64,128]{3,2,1,0:T(8,128)} custom-call(s32[2]{0:T(128)S(1)} %pad_add_fusion.place, bf16[1024,2048]{1,0:T(8,128)(2,1)} %get-tuple-element.34.natural, bf16[128,1792]{1,0:T(8,128)(2,1)S(1)} %copy-done, bf16[128,1792]{1,0:T(8,128)(2,1)S(1)} %collective-permute-done.10.refs_1_, bf16[128,1792]{1,0:T(8,128)(2,1)S(1)} %collective-permute-done.11.refs_2_, ...), custom_call_target="tpu_custom_call" | custom-call | flops 10000000000 | bytes 25165824 | tf_op jit(solution)/shard_map/pallas_call | solution.py:510
  (29 shorter events, 1.6 us)
Async XLA Ops:
  2.2 3.9 %collective-permute-start = (bf16[1,3,64,128]{3,2,1,0:T(8,128)(2,1)}, bf16[1,3,64,128]{3,2,1,0:T(8,128)(2,1)S(1)}, u32[]{:S(2)}, u32[]{:S(2)}) collective-permute-start(bf16[1,3,64,128]{3,2,1,0:T(8,128)(2,1)} %bitcast.26), channel_id=1, source_target_pairs={{0,1},{1,0},{2,3},{3,2},{4,5},{5,4},{6,7},{7,6},{8,9},{9,8},{10,11... | collective-permute-start | bytes 147464 | tf_op jit(solution)/shard_map/ppermute | solution.py:539
  6.8 4.5 %collective-permute-start.1 = (bf16[2,3,64,128]{3,2,1,0:T(8,128)(2,1)S(1)}, bf16[2,3,64,128]{3,2,1,0:T(8,128)(2,1)S(1)}, u32[]{:S(2)}, u32[]{:S(2)}) collective-permute-start(bf16[2,3,64,128]{3,2,1,0:T(8,128)(2,1)S(1)} %pad_maximum_fusion.5), channel_id=1, source_target_pairs={{0,2},{1,3},{2,0},{3,1},{4,6},{5,7},{6,4},{7,5},{8,10},{9,11},{10,... | collective-permute-start | bytes 294920 | tf_op jit(solution)/shard_map/ppermute | solution.py:539
  12.1 3.1 %collective-permute-start.2 = (bf16[1,4,1,64,128]{4,3,1,2,0:T(8,128)(2,1)S(1)}, bf16[1,4,1,64,128]{4,3,1,2,0:T(8,128)(2,1)S(1)}, u32[]{:S(2)}, u32[]{:S(2)}) collective-permute-start(bf16[1,4,1,64,128]{4,3,1,2,0:T(8,128)(2,1)S(1)} %maximum_bitcast_fusion), channel_id=1, source_target_pairs={{0,8},{4,12},{8,0},{12,4},{16,24},{20,28},{24,16},{28,20},{1,9},{5... | collective-permute-start | bytes 196616 | tf_op jit(solution)/shard_map/ppermute | solution.py:539
  15.3 3.9 %collective-permute-start.3 = (bf16[2,4,1,64,128]{4,3,1,2,0:T(8,128)(2,1)S(1)}, bf16[2,4,1,64,128]{4,3,1,2,0:T(8,128)(2,1)S(1)}, u32[]{:S(2)}, u32[]{:S(2)}) collective-permute-start(bf16[2,4,1,64,128]{4,3,1,2,0:T(8,128)(2,1)S(1)} %pad_maximum_fusion.4), channel_id=1, source_target_pairs={{0,16},{4,20},{8,24},{12,28},{16,0},{20,4},{24,8},{28,12},{1,17},{... | collective-permute-start | bytes 393224 | tf_op jit(solution)/shard_map/ppermute | solution.py:539
  19.2 16.8 %collective-permute-start.4 = (bf16[4,4,1,64,128]{4,3,1,2,0:T(8,128)(2,1)S(1)}, bf16[4,4,1,64,128]{4,3,1,2,0:T(8,128)(2,1)S(1)}, u32[]{:S(2)}, u32[]{:S(2)}) collective-permute-start(bf16[4,4,1,64,128]{4,3,1,2,0:T(8,128)(2,1)S(1)} %pad_maximum_fusion.2), channel_id=1, source_target_pairs={{0,4},{4,0},{8,12},{12,8},{16,20},{20,16},{24,28},{28,24},{1,5},{5... | collective-permute-start | bytes 786440 | tf_op jit(solution)/shard_map/ppermute | solution.py:539
  24.3 11.6 %copy-start.2 = (bf16[3,64,128]{2,1,0:T(8,128)(2,1)S(1)}, bf16[3,64,128]{2,1,0:T(8,128)(2,1)}, u32[]{:S(2)}) copy-start(bf16[3,64,128]{2,1,0:T(8,128)(2,1)} %get-tuple-element.35) | copy-start | bytes 147460
  36.0 25.2 %collective-permute-start.7 = (bf16[4,2,64,128]{3,2,1,0:T(8,128)(2,1)S(1)}, bf16[4,2,64,128]{3,2,1,0:T(8,128)(2,1)S(1)}, u32[]{:S(2)}, u32[]{:S(2)}) collective-permute-start(bf16[4,2,64,128]{3,2,1,0:T(8,128)(2,1)S(1)} %slice.8), channel_id=1, source_target_pairs={{0,24},{4,28},{8,16},{12,20},{16,8},{20,12},{24,0},{28,4},{1,25},{... | collective-permute-start | bytes 393224 | tf_op jit(solution)/shard_map/ppermute | solution.py:539
  38.5 22.8 %collective-permute-start.6 = (bf16[4,2,64,128]{3,2,1,0:T(8,128)(2,1)S(1)}, bf16[4,2,64,128]{3,2,1,0:T(8,128)(2,1)S(1)}, u32[]{:S(2)}, u32[]{:S(2)}) collective-permute-start(bf16[4,2,64,128]{3,2,1,0:T(8,128)(2,1)S(1)} %slice.8), channel_id=1, source_target_pairs={{0,16},{4,20},{8,24},{12,28},{16,0},{20,4},{24,8},{28,12},{1,17},{... | collective-permute-start | bytes 393224 | tf_op jit(solution)/shard_map/ppermute | solution.py:539
  38.7 22.5 %collective-permute-start.5 = (bf16[4,2,64,128]{3,2,1,0:T(8,128)(2,1)S(1)}, bf16[4,2,64,128]{3,2,1,0:T(8,128)(2,1)S(1)}, u32[]{:S(2)}, u32[]{:S(2)}) collective-permute-start(bf16[4,2,64,128]{3,2,1,0:T(8,128)(2,1)S(1)} %slice.8), channel_id=1, source_target_pairs={{0,8},{4,12},{8,0},{12,4},{16,24},{20,28},{24,16},{28,20},{1,9},{5... | collective-permute-start | bytes 393224 | tf_op jit(solution)/shard_map/ppermute | solution.py:539
  38.8 22.4 %collective-permute-start.9 = (bf16[896,256]{1,0:T(8,128)(2,1)}, bf16[896,256]{1,0:T(8,128)(2,1)S(1)}, u32[]{:S(2)}, u32[]{:S(2)}) collective-permute-start(bf16[896,256]{1,0:T(8,128)(2,1)} %get-tuple-element.50.refs_0_), channel_id=1, source_target_pairs={{0,3},{1,2},{2,1},{3,0},{4,7},{5,6},{6,5},{7,4},{8,11},{9,10},{10,... | collective-permute-start | bytes 1376264 | tf_op jit(solution)/shard_map/ppermute | solution.py:539
  43.2 21.1 %collective-permute-start.8 = (bf16[896,256]{1,0:T(8,128)(2,1)}, bf16[896,256]{1,0:T(8,128)(2,1)S(1)}, u32[]{:S(2)}, u32[]{:S(2)}) collective-permute-start(bf16[896,256]{1,0:T(8,128)(2,1)} %get-tuple-element.50.refs_0_), channel_id=1, source_target_pairs={{0,1},{1,0},{2,3},{3,2},{4,5},{5,4},{6,7},{7,6},{8,9},{9,8},{10,11... | collective-permute-start | bytes 1376264 | tf_op jit(solution)/shard_map/ppermute | solution.py:539
  43.2 21.8 %copy-start = (bf16[128,1792]{1,0:T(8,128)(2,1)S(1)}, bf16[128,1792]{1,0:T(8,128)(2,1)}, u32[]{:S(2)}) copy-start(bf16[128,1792]{1,0:T(8,128)(2,1)} %get-tuple-element.51.refs_0_) | copy-start | bytes 1376260
  43.2 24.4 %copy-start.1 = (bf16[896,256]{1,0:T(8,128)(2,1)S(1)}, bf16[896,256]{1,0:T(8,128)(2,1)}, u32[]{:S(2)}) copy-start(bf16[896,256]{1,0:T(8,128)(2,1)} %get-tuple-element.50.refs_0_) | copy-start | bytes 1376260
  64.4 3.5 %collective-permute-start.13 = (bf16[4,4,2,64,128]{4,3,2,1,0:T(8,128)(2,1)S(1)}, bf16[4,4,2,64,128]{4,3,2,1,0:T(8,128)(2,1)S(1)}, u32[]{:S(2)}, u32[]{:S(2)}) collective-permute-start(bf16[4,4,2,64,128]{4,3,2,1,0:T(8,128)(2,1)S(1)} %pad_maximum_fusion.1.near), channel_id=1, source_target_pairs={{0,4},{4,0},{8,12},{12,8},{16,20},{20,16},{24,28},{28,24},{1,5},{5... | collective-permute-start | bytes 1572872 | tf_op jit(solution)/shard_map/ppermute | solution.py:539
  64.9 24.7 %collective-permute-start.12 = (bf16[128,1792]{1,0:T(8,128)(2,1)S(1)}, bf16[128,1792]{1,0:T(8,128)(2,1)S(1)}, u32[]{:S(2)}, u32[]{:S(2)}) collective-permute-start(bf16[128,1792]{1,0:T(8,128)(2,1)S(1)} %copy-done), channel_id=1, source_target_pairs={{0,24},{4,28},{8,16},{12,20},{16,8},{20,12},{24,0},{28,4},{1,25},{... | collective-permute-start | bytes 1376264 | tf_op jit(solution)/shard_map/ppermute | solution.py:539
  67.1 22.5 %collective-permute-start.11 = (bf16[128,1792]{1,0:T(8,128)(2,1)S(1)}, bf16[128,1792]{1,0:T(8,128)(2,1)S(1)}, u32[]{:S(2)}, u32[]{:S(2)}) collective-permute-start(bf16[128,1792]{1,0:T(8,128)(2,1)S(1)} %copy-done), channel_id=1, source_target_pairs={{0,16},{4,20},{8,24},{12,28},{16,0},{20,4},{24,8},{28,12},{1,17},{... | collective-permute-start | bytes 1376264 | tf_op jit(solution)/shard_map/ppermute | solution.py:539
  67.4 22.3 %collective-permute-start.10 = (bf16[128,1792]{1,0:T(8,128)(2,1)S(1)}, bf16[128,1792]{1,0:T(8,128)(2,1)S(1)}, u32[]{:S(2)}, u32[]{:S(2)}) collective-permute-start(bf16[128,1792]{1,0:T(8,128)(2,1)S(1)} %copy-done), channel_id=1, source_target_pairs={{0,8},{4,12},{8,0},{12,4},{16,24},{20,28},{24,16},{28,20},{1,9},{5... | collective-permute-start | bytes 1376264 | tf_op jit(solution)/shard_map/ppermute | solution.py:539
  67.6 22.0 %collective-permute-start.14 = (bf16[896,256]{1,0:T(8,128)(2,1)S(1)}, bf16[896,256]{1,0:T(8,128)(2,1)S(1)}, u32[]{:S(2)}, u32[]{:S(2)}) collective-permute-start(bf16[896,256]{1,0:T(8,128)(2,1)S(1)} %copy-done.1), channel_id=1, source_target_pairs={{0,2},{1,3},{2,0},{3,1},{4,6},{5,7},{6,4},{7,5},{8,10},{9,11},{10,... | collective-permute-start | bytes 1376264 | tf_op jit(solution)/shard_map/ppermute | solution.py:539
  89.9 6.8 %collective-permute-start.15 = (bf16[4,128,1792]{2,1,0:T(8,128)(2,1)S(1)}, bf16[4,128,1792]{2,1,0:T(8,128)(2,1)S(1)}, u32[]{:S(2)}, u32[]{:S(2)}) collective-permute-start(bf16[4,128,1792]{2,1,0:T(8,128)(2,1)S(1)} %pad_maximum_fusion), channel_id=1, source_target_pairs={{0,4},{4,0},{8,12},{12,8},{16,20},{20,16},{24,28},{28,24},{1,5},{5... | collective-permute-start | bytes 5505032 | tf_op jit(solution)/shard_map/ppermute | solution.py:539

commit v3 on v2

--- a/solution.py
+++ b/solution.py
@@ -253,13 +253,18 @@
 
 
 def natural_kernel(tiles, natural, left, spread_rows):
-    tile_rows = natural.shape[0]
-    natural_tile(tiles[0], spread_rows, tile_rows)
-    for s in range(NT):
-        tile = spread_rows[pl.ds(s, tile_rows, stride=NT), :].astype(jnp.bfloat16)
-        natural[:, s * BLOCK : (s + 1) * BLOCK] = tile
-        if s < 2:
-            left[:, s * BLOCK : (s + 1) * BLOCK] = tile
+    group = tiles.shape[0]
+    tile_rows = natural.shape[0] // group
+    step = pl.program_id(0)
+    for t in range(group):
+        natural_tile(tiles[t], spread_rows, tile_rows)
+        rows = slice(t * tile_rows, (t + 1) * tile_rows)
+        for s in range(NT):
+            tile = spread_rows[pl.ds(s, tile_rows, stride=NT), :].astype(jnp.bfloat16)
+            natural[rows, s * BLOCK : (s + 1) * BLOCK] = tile
+            if s < 2:
+                first = pl.multiple_of(jnp.maximum(step * group + t - 2, 0) * tile_rows, tile_rows)
+                left[pl.ds(first, tile_rows), s * BLOCK : (s + 1) * BLOCK] = tile
 
 
 def take_top(tiles, tile_rows):
@@ -275,25 +280,27 @@
             pltpu.VMEM((tile_rows * NT, BLOCK), jnp.float32),
             pltpu.SemaphoreType.DMA((2,)),
         ],
-        compiler_params=pltpu.CompilerParams(vmem_limit_bytes=60 * 2**20),
+        compiler_params=pltpu.CompilerParams(vmem_limit_bytes=16 * 2**20),
     )(tiles)
 
 
 def take_natural(tiles, tile_rows):
+    group = 4
+    below = ((NT - 2) * tile_rows, 2 * BLOCK)
     return pl.pallas_call(
         natural_kernel,
-        grid=(NT,),
-        in_specs=[pl.BlockSpec((1, NT, tile_rows * BLOCK), lambda t: (t, 0, 0))],
+        grid=(NT // group,),
+        in_specs=[pl.BlockSpec((group, NT, tile_rows * BLOCK), lambda t: (t, 0, 0))],
         out_specs=[
-            pl.BlockSpec((tile_rows, NT * BLOCK), lambda t: (t, 0)),
-            pl.BlockSpec((tile_rows, 2 * BLOCK), lambda t: (jnp.maximum(t - 2, 0), 0)),
+            pl.BlockSpec((group * tile_rows, NT * BLOCK), lambda t: (t, 0)),
+            whole(below),
         ],
         out_shape=[
             jax.ShapeDtypeStruct((NT * tile_rows, NT * BLOCK), jnp.bfloat16),
-            jax.ShapeDtypeStruct(((NT - 2) * tile_rows, 2 * BLOCK), jnp.bfloat16),
+            jax.ShapeDtypeStruct(below, jnp.bfloat16),
         ],
         scratch_shapes=[pltpu.VMEM((tile_rows * NT, BLOCK), jnp.float32)],
-        compiler_params=pltpu.CompilerParams(vmem_limit_bytes=60 * 2**20),
+        compiler_params=pltpu.CompilerParams(vmem_limit_bytes=16 * 2**20),
         cost_estimate=pl.CostEstimate(
             flops=0, bytes_accessed=16 * NT * tile_rows * NT * BLOCK, transcendentals=0
         ),
@@ -395,7 +402,7 @@
 
 def solve_rows(place, lefts, first_inverse, second_inverse, cross):
     count = lefts[0].shape[0]
-    rows = count // 2
+    rows = count
     square = whole((P_SIZE, P_SIZE))
     return pl.pallas_call(
         rows_kernel,
@@ -430,12 +437,13 @@
     evens, odds = refs[:chips], refs[chips]
     first_factor, first_inverse, second_factor, second_inverse, cross = refs[chips + 1 : chips + 6]
     rounded, own, own_cross, result = refs[chips + 6 : chips + 10]
-    given_cols, first_side, second_side, copied = refs[chips + 10 :]
+    given_cols, solved_cols, first_side, second_side, copied = refs[chips + 10 :]
     row_index, column_index = place[0], place[1]
     tile_rows = evens[0].shape[0] // 2
-    order, half = P_SIZE, P_SIZE // 2
+    order = P_SIZE
     step = pl.program_id(0)
-    width = 2 * BLOCK
+    group = result.shape[1]
+    count = given_cols.shape[1]
 
     def copies():
         for chip in range(chips):
@@ -448,6 +456,20 @@
                         given_cols.at[pl.ds(t * order + first, tile_rows), :],
                         copied.at[(2 * chip + core) * 2 + t],
                     )
+
+    def write(first_col, tile_cols):
+        here = pl.ds(pl.multiple_of(first_col, BLOCK), tile_cols * BLOCK)
+        skipped = (group - tile_cols) * BLOCK
+        product = fast_dot(rounded[...], solved_cols[:, here])
+        kept = natural[2 * tile_rows :, skipped:].astype(jnp.float32) - product
+        for s in range(tile_cols):
+            at = group - tile_cols + s
+            for t in range(2):
+                result[t, at] = jnp.zeros((tile_rows, BLOCK), jnp.float32)
+            for t in range(2, NT):
+                result[t, at] = kept[
+                    (t - 2) * tile_rows : (t - 1) * tile_rows, s * BLOCK : (s + 1) * BLOCK
+                ]
 
     @pl.when(step == 0)
     def _():
@@ -473,61 +495,53 @@
             result[t, 1] = own[rows, BLOCK:]
         for copy in copies():
             copy.wait()
+        begin = 0
+        while begin < count:
+            width = min(1024, count - begin)
+            here = slice(begin, begin + width)
+            begin += width
+            given = given_cols[0:order, here]
+            first = fast_dot(first_side[...], jnp.concatenate([given, given]))
+            first = first.astype(jnp.bfloat16)
+            solved_cols[0:order, here] = first
+            left_over = given_cols[order:, here].astype(jnp.float32) - fast_dot(cross[...], first)
+            high, low = split(left_over)
+            second = fast_dot(second_side[...], jnp.concatenate([high, low, high]))
+            solved_cols[order:, here] = second.astype(jnp.bfloat16)
+        write(0, group - 2)
 
     @pl.when(step > 0)
     def _():
-        here = pl.ds(pl.multiple_of((step - 1) * width, width), width)
-
-        def lower_dot(side, parts):
-            upper_side = jnp.concatenate(
-                [side[0:half, k * order : k * order + half] for k in range(len(parts))], axis=1
-            )
-            upper = fast_dot(upper_side, jnp.concatenate([part[0:half] for part in parts]))
-            lower = fast_dot(side[half:order, :], jnp.concatenate(parts))
-            return jnp.concatenate([upper, lower])
-
-        given = given_cols[0:order, here]
-        first = lower_dot(first_side, [given, given]).astype(jnp.bfloat16)
-        left_over = given_cols[order:, here].astype(jnp.float32) - fast_dot(cross[...], first)
-        high, low = split(left_over)
-        second = lower_dot(second_side, [high, low, high]).astype(jnp.bfloat16)
-        begin = 2 * tile_rows
-        product = fast_dot(rounded[...], jnp.concatenate([first, second]))
-        kept = natural[begin:, :].astype(jnp.float32) - product
-        for s in range(2):
-            for t in range(NT):
-                if t < 2:
-                    result[t, s] = jnp.zeros((tile_rows, BLOCK), jnp.float32)
-                else:
-                    result[t, s] = kept[
-                        (t - 2) * tile_rows : (t - 1) * tile_rows, s * BLOCK : (s + 1) * BLOCK
-                    ]
+        write((step * group - 2) * BLOCK, group)
 
 
 def solve_cols(place, natural, evens, odds, factors, rounded, own, own_cross, tile_rows):
     chips = len(evens)
+    group = 4
     square = whole((P_SIZE, P_SIZE))
+    solved = pltpu.VMEM((2 * P_SIZE, (NT - 2) * BLOCK), jnp.bfloat16)
     return pl.pallas_call(
         functools.partial(cols_kernel, chips),
-        grid=(NT // 2,),
+        grid=(NT // group,),
         in_specs=[
             pl.BlockSpec(memory_space=pltpu.SMEM),
-            pl.BlockSpec((NT * tile_rows, 2 * BLOCK), lambda j: (0, j)),
+            pl.BlockSpec((NT * tile_rows, group * BLOCK), lambda j: (0, j)),
             *[pl.BlockSpec(memory_space=pl.ANY)] * (chips + 1),
             *[square] * 5,
             whole(rounded.shape),
             whole(own.shape),
             whole(own_cross.shape),
         ],
-        out_specs=pl.BlockSpec((NT, 2, tile_rows, BLOCK), lambda j: (0, j, 0, 0)),
+        out_specs=pl.BlockSpec((NT, group, tile_rows, BLOCK), lambda j: (0, j, 0, 0)),
         out_shape=jax.ShapeDtypeStruct((NT, NT, tile_rows, BLOCK), jnp.float32),
         scratch_shapes=[
-            pltpu.VMEM((2 * P_SIZE, (NT - 2) * BLOCK), jnp.bfloat16),
+            solved,
+            solved,
             pltpu.VMEM((P_SIZE, 2 * P_SIZE), jnp.bfloat16),
             pltpu.VMEM((P_SIZE, 3 * P_SIZE), jnp.bfloat16),
             pltpu.SemaphoreType.DMA((4 * chips,)),
         ],
-        compiler_params=pltpu.CompilerParams(vmem_limit_bytes=40 * 2**20),
+        compiler_params=pltpu.CompilerParams(vmem_limit_bytes=38 * 2**20),
         cost_estimate=pl.CostEstimate(
             flops=10 * 10**9, bytes_accessed=24 * 2**20, transcendentals=0
         ),

time: 117 us -> 106 us (0.906)
  Pallas kernels: 75.5 us -> 62.7 us
  local copies, waits for them, and re-layouts: 0.02 us -> 4.21 us
  other arithmetic: 1.97 us -> 0.46 us
    pallas_call x2, Pallas kernels: 31 us -> 20.8 us  [the longest x1 17.6 us: solve_cols(): pl.pallas_call(functools.partial(cols_kernel, chips), grid=(NT // group,)...]
    unnamed x6, local copies, waits for them, and re-layouts: 0.01 us -> 4.2 us
    pallas_call x1, Pallas kernels: 2.14 us -> 0.46 us  [take_top(): pl.pallas_call(top_kernel, in_specs=[pl.BlockSpec(memory_space=pltpu.HBM)...]
  transfers between devices with their start and end apart: 16 -> 16, of which waited for: 6 -> 6; matrix products, arithmetic and copies ran while one was open for 0% -> 0% of each run, Pallas kernels for 46% -> 42%
where the time goes in v3:
time: 106 us
  Pallas kernels  62.7 us (59%)
  starting transfers between devices  25 us (24%)
  waiting for transfers between devices  13.2 us (12%)
  local copies, waits for them, and re-layouts  4.21 us (4%)
    pallas_call x2, Pallas kernels, factor_call(): pl.pallas_call(body, in_specs=[pl.BlockSpec(memory_space=pltpu.SMEM)] + [...  37.3 us
    ppermute x16, starting transfers between devices, swap(): return lax.ppermute(value, axis, [(i, i ^ offset) for i in range(count)])  25 us
    pallas_call x1, Pallas kernels, solve_cols(): pl.pallas_call(functools.partial(cols_kernel, chips), grid=(NT // group,)...  17.6 us
    ppermute x16, waiting for transfers between devices, swap(): return lax.ppermute(value, axis, [(i, i ^ offset) for i in range(count)])  13.2 us
    unnamed x6, local copies, waits for them, and re-layouts  4.2 us
    pallas_call x1, Pallas kernels, solve_rows(): pl.pallas_call(rows_kernel, grid=(count // rows,), in_specs=[pl.BlockSpec...  4.16 us
    pallas_call x1, Pallas kernels, take_natural(): pl.pallas_call(natural_kernel, grid=(NT // group,), in_specs=[pl.BlockSpe...  3.26 us
  transfers between devices with their start and end apart: 16, of which 6 were waited for; matrix products, arithmetic and copies ran while one was open for 0% of the time, Pallas kernels for 42%

profile of v3, /device:TPU:1, one launch (start us, length us, event | category | flops | bytes accessed | tf_op | source)
XLA Modules:
  0.0 105.9 jit_solution(962423597454385604)
XLA Ops:
  0.0 2.2 %copy-done = bf16[16,1,16,1,8192]{4,2,3,1,0:T(8,128)(2,1)S(1)} copy-done((bf16[16,1,16,1,8192]{4,2,3,1,0:T(8,128)(2,1)S(1)}, bf16[16,1,16,1,8192]{4,2,3,1,0:T(8,128)(2,1)}, u32[]{:S(2)}) %copy-start) | copy-done | bytes 4194328
  2.2 0.5 shard_map.18
  2.7 2.2 %collective-permute-start = (bf16[1,3,64,128]{3,2,1,0:T(8,128)(2,1)S(1)}, bf16[1,3,64,128]{3,2,1,0:T(8,128)(2,1)S(1)}, u32[]{:S(2)}, u32[]{:S(2)}) collective-permute-start(bf16[1,3,64,128]{3,2,1,0:T(8,128)(2,1)S(1)} %bitcast.23), channel_id=1, source_target_pairs={{0,1},{1,0},{2,3},{3,2},{4,5},{5,4},{6,7},{7,6},{8,9},{9,8},{10,11... | collective-permute-start | bytes 147464 | tf_op jit(solution)/shard_map/ppermute | solution.py:553
  4.8 1.5 %collective-permute-done = bf16[1,3,64,128]{3,2,1,0:T(8,128)(2,1)S(1)} collective-permute-done((bf16[1,3,64,128]{3,2,1,0:T(8,128)(2,1)S(1)}, bf16[1,3,64,128]{3,2,1,0:T(8,128)(2,1)S(1)}, u32[]{:S(2)}, u32[]{:S(2)}) %collective-permute-start) | collective-permute-done | bytes 49184 | tf_op jit(solution)/shard_map/ppermute | solution.py:553
  6.3 2.5 %collective-permute-start.1 = (bf16[2,3,64,128]{3,2,1,0:T(8,128)(2,1)S(1)}, bf16[2,3,64,128]{3,2,1,0:T(8,128)(2,1)S(1)}, u32[]{:S(2)}, u32[]{:S(2)}) collective-permute-start(bf16[2,3,64,128]{3,2,1,0:T(8,128)(2,1)S(1)} %pad_maximum_fusion.5), channel_id=1, source_target_pairs={{0,2},{1,3},{2,0},{3,1},{4,6},{5,7},{6,4},{7,5},{8,10},{9,11},{10,... | collective-permute-start | bytes 294920 | tf_op jit(solution)/shard_map/ppermute | solution.py:553
  8.9 2.0 %collective-permute-done.1 = bf16[2,3,64,128]{3,2,1,0:T(8,128)(2,1)S(1)} collective-permute-done((bf16[2,3,64,128]{3,2,1,0:T(8,128)(2,1)S(1)}, bf16[2,3,64,128]{3,2,1,0:T(8,128)(2,1)S(1)}, u32[]{:S(2)}, u32[]{:S(2)}) %collective-permute-start.1) | collective-permute-done | bytes 98336 | tf_op jit(solution)/shard_map/ppermute | solution.py:553
  10.9 1.3 %collective-permute-start.2 = (bf16[1,4,1,64,128]{4,3,1,2,0:T(8,128)(2,1)S(1)}, bf16[1,4,1,64,128]{4,3,1,2,0:T(8,128)(2,1)S(1)}, u32[]{:S(2)}, u32[]{:S(2)}) collective-permute-start(bf16[1,4,1,64,128]{4,3,1,2,0:T(8,128)(2,1)S(1)} %maximum_bitcast_fusion), channel_id=1, source_target_pairs={{0,8},{4,12},{8,0},{12,4},{16,24},{20,28},{24,16},{28,20},{1,9},{5... | collective-permute-start | bytes 196616 | tf_op jit(solution)/shard_map/ppermute | solution.py:553
  12.2 1.8 %collective-permute-done.2 = bf16[1,4,1,64,128]{4,3,1,2,0:T(8,128)(2,1)S(1)} collective-permute-done((bf16[1,4,1,64,128]{4,3,1,2,0:T(8,128)(2,1)S(1)}, bf16[1,4,1,64,128]{4,3,1,2,0:T(8,128)(2,1)S(1)}, u32[]{:S(2)}, u32[]{:S(2)}) %collective-permute-start.2) | collective-permute-done | bytes 65568 | tf_op jit(solution)/shard_map/ppermute | solution.py:553
  14.1 1.4 %collective-permute-start.3 = (bf16[2,4,1,64,128]{4,3,1,2,0:T(8,128)(2,1)S(1)}, bf16[2,4,1,64,128]{4,3,1,2,0:T(8,128)(2,1)S(1)}, u32[]{:S(2)}, u32[]{:S(2)}) collective-permute-start(bf16[2,4,1,64,128]{4,3,1,2,0:T(8,128)(2,1)S(1)} %pad_maximum_fusion.4), channel_id=1, source_target_pairs={{0,16},{4,20},{8,24},{12,28},{16,0},{20,4},{24,8},{28,12},{1,17},{... | collective-permute-start | bytes 393224 | tf_op jit(solution)/shard_map/ppermute | solution.py:553
  15.5 2.5 %collective-permute-done.3 = bf16[2,4,1,64,128]{4,3,1,2,0:T(8,128)(2,1)S(1)} collective-permute-done((bf16[2,4,1,64,128]{4,3,1,2,0:T(8,128)(2,1)S(1)}, bf16[2,4,1,64,128]{4,3,1,2,0:T(8,128)(2,1)S(1)}, u32[]{:S(2)}, u32[]{:S(2)}) %collective-permute-start.3) | collective-permute-done | bytes 131104 | tf_op jit(solution)/shard_map/ppermute | solution.py:553
  18.0 5.2 %collective-permute-start.4 = (bf16[4,4,1,64,128]{4,3,1,2,0:T(8,128)(2,1)S(1)}, bf16[4,4,1,64,128]{4,3,1,2,0:T(8,128)(2,1)S(1)}, u32[]{:S(2)}, u32[]{:S(2)}) collective-permute-start(bf16[4,4,1,64,128]{4,3,1,2,0:T(8,128)(2,1)S(1)} %pad_maximum_fusion.2), channel_id=1, source_target_pairs={{0,4},{4,0},{8,12},{12,8},{16,20},{20,16},{24,28},{28,24},{1,5},{5... | collective-permute-start | bytes 786440 | tf_op jit(solution)/shard_map/ppermute | solution.py:553
  23.2 3.3 %shard_map.17 = (bf16[1024,2048]{1,0:T(8,128)(2,1)S(1)}, bf16[896,256]{1,0:T(8,128)(2,1)S(1)}) custom-call(bf16[16,16,8192]{2,1,0:T(8,128)(2,1)S(1)} %bitcast.18), custom_call_target="tpu_custom_call" | custom-call | bytes 33554432 | tf_op jit(solution)/shard_map/pallas_call | solution.py:290
  26.5 2.0 %copy-done.1 = bf16[1024,2048]{1,0:T(8,128)(2,1)} copy-done((bf16[1024,2048]{1,0:T(8,128)(2,1)}, bf16[1024,2048]{1,0:T(8,128)(2,1)S(1)}, u32[]{:S(2)}) %copy-start.1) | copy-done | bytes 4194328
  28.6 2.5 %collective-permute-start.7 = (bf16[4,2,64,128]{3,2,1,0:T(8,128)(2,1)S(1)}, bf16[4,2,64,128]{3,2,1,0:T(8,128)(2,1)S(1)}, u32[]{:S(2)}, u32[]{:S(2)}) collective-permute-start(bf16[4,2,64,128]{3,2,1,0:T(8,128)(2,1)S(1)} %slice.8), channel_id=1, source_target_pairs={{0,24},{4,28},{8,16},{12,20},{16,8},{20,12},{24,0},{28,4},{1,25},{... | collective-permute-start | bytes 393224 | tf_op jit(solution)/shard_map/ppermute | solution.py:553
  31.4 4.4 %collective-permute-start.9 = (bf16[896,256]{1,0:T(8,128)(2,1)S(1)}, bf16[896,256]{1,0:T(8,128)(2,1)S(1)}, u32[]{:S(2)}, u32[]{:S(2)}) collective-permute-start(bf16[896,256]{1,0:T(8,128)(2,1)S(1)} %get-tuple-element.50.refs_0_), channel_id=1, source_target_pairs={{0,3},{1,2},{2,1},{3,0},{4,7},{5,6},{6,5},{7,4},{8,11},{9,10},{10,... | collective-permute-start | bytes 1376264 | tf_op jit(solution)/shard_map/ppermute | solution.py:553
  35.8 18.0 %shard_map.19 = (f32[512,512]{1,0:T(8,128)S(1)}, f32[512,512]{1,0:T(8,128)S(1)}) custom-call(s32[2]{0:T(128)S(1)} %pad_add_fusion.place, bf16[4,4,1,64,128]{4,3,2,1,0:T(8,128)(2,1)S(1)} %bitcast.27, bf16[4,4,1,64,128]{4,3,2,1,0:T(8,128)(2,1)S(1)} %bitcast.28), custom_call_target="tpu_custom_call" | custom-call | flops 40000000000 | bytes 4194304 | tf_op jit(solution)/shard_map/pallas_call | solution.py:355
  53.8 2.9 %collective-permute-done.8.refs_1_ = bf16[896,256]{1,0:T(8,128)(2,1)S(1)} collective-permute-done((bf16[896,256]{1,0:T(8,128)(2,1)S(1)}, bf16[896,256]{1,0:T(8,128)(2,1)S(1)}, u32[]{:S(2)}, u32[]{:S(2)}) %collective-permute-start.8) | collective-permute-done | bytes 458784 | tf_op jit(solution)/shard_map/ppermute | solution.py:553
  56.8 0.6 collective-permute-start.13
  57.3 2.2 %collective-permute-start.12 = (bf16[128,1792]{1,0:T(8,128)(2,1)S(1)}, bf16[128,1792]{1,0:T(8,128)(2,1)S(1)}, u32[]{:S(2)}, u32[]{:S(2)}) collective-permute-start(bf16[128,1792]{1,0:T(8,128)(2,1)S(1)} %get-tuple-element.51.refs_0_), channel_id=1, source_target_pairs={{0,24},{4,28},{8,16},{12,20},{16,8},{20,12},{24,0},{28,4},{1,25},{... | collective-permute-start | bytes 1376264 | tf_op jit(solution)/shard_map/ppermute | solution.py:553
  60.3 19.3 %shard_map.20 = (f32[512,512]{1,0:T(8,128)S(1)}, f32[512,512]{1,0:T(8,128)S(1)}, bf16[512,512]{1,0:T(8,128)(2,1)S(1)}, f32[64,128]{1,0:T(8,128)S(1)}) custom-call(s32[2]{0:T(128)S(1)} %pad_add_fusion.place, bf16[4,4,2,64,128]{4,3,2,1,0:T(8,128)(2,1)S(1)} %pad_maximum_fusion.1.near, bf16[4,4,2,64,128]{4,3,2,1,0:T(8,128)(2,1)S(1)} %collective-permute-done.13.far, ...), custom_call_target="tpu_custom_call" | custom-call | flops 40000000000 | bytes 4194304 | tf_op jit(solution)/shard_map/pallas_call | solution.py:355
  79.5 2.4 %collective-permute-done.14.refs_2_ = bf16[896,256]{1,0:T(8,128)(2,1)S(1)} collective-permute-done((bf16[896,256]{1,0:T(8,128)(2,1)S(1)}, bf16[896,256]{1,0:T(8,128)(2,1)S(1)}, u32[]{:S(2)}, u32[]{:S(2)}) %collective-permute-start.14) | collective-permute-done | bytes 458784 | tf_op jit(solution)/shard_map/ppermute | solution.py:553
  82.2 1.7 %collective-permute-start.15 = (bf16[4,128,1792]{2,1,0:T(8,128)(2,1)S(1)}, bf16[4,128,1792]{2,1,0:T(8,128)(2,1)S(1)}, u32[]{:S(2)}, u32[]{:S(2)}) collective-permute-start(bf16[4,128,1792]{2,1,0:T(8,128)(2,1)S(1)} %pad_maximum_fusion), channel_id=1, source_target_pairs={{0,4},{4,0},{8,12},{12,8},{16,20},{20,16},{24,28},{28,24},{1,5},{5... | collective-permute-start | bytes 5505032 | tf_op jit(solution)/shard_map/ppermute | solution.py:553
  84.0 4.2 %shard_map.21 = (bf16[896,1024]{1,0:T(8,128)(2,1)S(1)}, f32[896,256]{1,0:T(8,128)S(1)}) custom-call(s32[2]{0:T(128)S(1)} %pad_add_fusion.place, bf16[896,256]{1,0:T(8,128)(2,1)S(1)} %get-tuple-element.50.refs_0_, bf16[896,256]{1,0:T(8,128)(2,1)S(1)} %collective-permute-done.8.refs_1_, bf16[896,256]{1,0:T(8,128)(2,1)S(1)} %collective-permute-done.14.refs_2_, ...), custom_call_target="tpu_custom_call" | custom-call | flops 2818572288 | bytes 10485760 | tf_op jit(solution)/shard_map/pallas_call | solution.py:407
  88.2 17.6 %shard_map.22 = f32[16,16,64,128]{3,2,1,0:T(8,128)} custom-call(s32[2]{0:T(128)S(1)} %pad_add_fusion.place, bf16[1024,2048]{1,0:T(8,128)(2,1)S(1)} %copy-done.2, bf16[128,1792]{1,0:T(8,128)(2,1)S(1)} %get-tuple-element.51.refs_0_, bf16[128,1792]{1,0:T(8,128)(2,1)S(1)} %collective-permute-done.10.refs_1_, ...), custom_call_target="tpu_custom_call" | custom-call | flops 10000000000 | bytes 25165824 | tf_op jit(solution)/shard_map/pallas_call | solution.py:523
  (29 shorter events, 1.6 us)
Async XLA Ops:
  0.0 2.2 %copy-start = (bf16[16,1,16,1,8192]{4,2,3,1,0:T(8,128)(2,1)S(1)}, bf16[16,1,16,1,8192]{4,2,3,1,0:T(8,128)(2,1)}, u32[]{:S(2)}) copy-start(bf16[16,1,16,1,8192]{4,2,3,1,0:T(8,128)(2,1)} %param.1) | copy-start | bytes 12582916
  2.7 3.7 %collective-permute-start = (bf16[1,3,64,128]{3,2,1,0:T(8,128)(2,1)S(1)}, bf16[1,3,64,128]{3,2,1,0:T(8,128)(2,1)S(1)}, u32[]{:S(2)}, u32[]{:S(2)}) collective-permute-start(bf16[1,3,64,128]{3,2,1,0:T(8,128)(2,1)S(1)} %bitcast.23), channel_id=1, source_target_pairs={{0,1},{1,0},{2,3},{3,2},{4,5},{5,4},{6,7},{7,6},{8,9},{9,8},{10,11... | collective-permute-start | bytes 147464 | tf_op jit(solution)/shard_map/ppermute | solution.py:553
  6.3 4.5 %collective-permute-start.1 = (bf16[2,3,64,128]{3,2,1,0:T(8,128)(2,1)S(1)}, bf16[2,3,64,128]{3,2,1,0:T(8,128)(2,1)S(1)}, u32[]{:S(2)}, u32[]{:S(2)}) collective-permute-start(bf16[2,3,64,128]{3,2,1,0:T(8,128)(2,1)S(1)} %pad_maximum_fusion.5), channel_id=1, source_target_pairs={{0,2},{1,3},{2,0},{3,1},{4,6},{5,7},{6,4},{7,5},{8,10},{9,11},{10,... | collective-permute-start | bytes 294920 | tf_op jit(solution)/shard_map/ppermute | solution.py:553
  10.9 3.2 %collective-permute-start.2 = (bf16[1,4,1,64,128]{4,3,1,2,0:T(8,128)(2,1)S(1)}, bf16[1,4,1,64,128]{4,3,1,2,0:T(8,128)(2,1)S(1)}, u32[]{:S(2)}, u32[]{:S(2)}) collective-permute-start(bf16[1,4,1,64,128]{4,3,1,2,0:T(8,128)(2,1)S(1)} %maximum_bitcast_fusion), channel_id=1, source_target_pairs={{0,8},{4,12},{8,0},{12,4},{16,24},{20,28},{24,16},{28,20},{1,9},{5... | collective-permute-start | bytes 196616 | tf_op jit(solution)/shard_map/ppermute | solution.py:553
  14.1 3.9 %collective-permute-start.3 = (bf16[2,4,1,64,128]{4,3,1,2,0:T(8,128)(2,1)S(1)}, bf16[2,4,1,64,128]{4,3,1,2,0:T(8,128)(2,1)S(1)}, u32[]{:S(2)}, u32[]{:S(2)}) collective-permute-start(bf16[2,4,1,64,128]{4,3,1,2,0:T(8,128)(2,1)S(1)} %pad_maximum_fusion.4), channel_id=1, source_target_pairs={{0,16},{4,20},{8,24},{12,28},{16,0},{20,4},{24,8},{28,12},{1,17},{... | collective-permute-start | bytes 393224 | tf_op jit(solution)/shard_map/ppermute | solution.py:553
  18.0 10.6 %collective-permute-start.4 = (bf16[4,4,1,64,128]{4,3,1,2,0:T(8,128)(2,1)S(1)}, bf16[4,4,1,64,128]{4,3,1,2,0:T(8,128)(2,1)S(1)}, u32[]{:S(2)}, u32[]{:S(2)}) collective-permute-start(bf16[4,4,1,64,128]{4,3,1,2,0:T(8,128)(2,1)S(1)} %pad_maximum_fusion.2), channel_id=1, source_target_pairs={{0,4},{4,0},{8,12},{12,8},{16,20},{20,16},{24,28},{28,24},{1,5},{5... | collective-permute-start | bytes 786440 | tf_op jit(solution)/shard_map/ppermute | solution.py:553
  26.4 2.0 %copy-start.1 = (bf16[1024,2048]{1,0:T(8,128)(2,1)}, bf16[1024,2048]{1,0:T(8,128)(2,1)S(1)}, u32[]{:S(2)}) copy-start(bf16[1024,2048]{1,0:T(8,128)(2,1)S(1)} %get-tuple-element.34.natural) | copy-start | bytes 12582916
  28.6 25.2 %collective-permute-start.7 = (bf16[4,2,64,128]{3,2,1,0:T(8,128)(2,1)S(1)}, bf16[4,2,64,128]{3,2,1,0:T(8,128)(2,1)S(1)}, u32[]{:S(2)}, u32[]{:S(2)}) collective-permute-start(bf16[4,2,64,128]{3,2,1,0:T(8,128)(2,1)S(1)} %slice.8), channel_id=1, source_target_pairs={{0,24},{4,28},{8,16},{12,20},{16,8},{20,12},{24,0},{28,4},{1,25},{... | collective-permute-start | bytes 393224 | tf_op jit(solution)/shard_map/ppermute | solution.py:553
  31.1 22.8 %collective-permute-start.6 = (bf16[4,2,64,128]{3,2,1,0:T(8,128)(2,1)S(1)}, bf16[4,2,64,128]{3,2,1,0:T(8,128)(2,1)S(1)}, u32[]{:S(2)}, u32[]{:S(2)}) collective-permute-start(bf16[4,2,64,128]{3,2,1,0:T(8,128)(2,1)S(1)} %slice.8), channel_id=1, source_target_pairs={{0,16},{4,20},{8,24},{12,28},{16,0},{20,4},{24,8},{28,12},{1,17},{... | collective-permute-start | bytes 393224 | tf_op jit(solution)/shard_map/ppermute | solution.py:553
  31.3 22.5 %collective-permute-start.5 = (bf16[4,2,64,128]{3,2,1,0:T(8,128)(2,1)S(1)}, bf16[4,2,64,128]{3,2,1,0:T(8,128)(2,1)S(1)}, u32[]{:S(2)}, u32[]{:S(2)}) collective-permute-start(bf16[4,2,64,128]{3,2,1,0:T(8,128)(2,1)S(1)} %slice.8), channel_id=1, source_target_pairs={{0,8},{4,12},{8,0},{12,4},{16,24},{20,28},{24,16},{28,20},{1,9},{5... | collective-permute-start | bytes 393224 | tf_op jit(solution)/shard_map/ppermute | solution.py:553
  31.4 22.4 %collective-permute-start.9 = (bf16[896,256]{1,0:T(8,128)(2,1)S(1)}, bf16[896,256]{1,0:T(8,128)(2,1)S(1)}, u32[]{:S(2)}, u32[]{:S(2)}) collective-permute-start(bf16[896,256]{1,0:T(8,128)(2,1)S(1)} %get-tuple-element.50.refs_0_), channel_id=1, source_target_pairs={{0,3},{1,2},{2,1},{3,0},{4,7},{5,6},{6,5},{7,4},{8,11},{9,10},{10,... | collective-permute-start | bytes 1376264 | tf_op jit(solution)/shard_map/ppermute | solution.py:553
  35.8 20.9 %collective-permute-start.8 = (bf16[896,256]{1,0:T(8,128)(2,1)S(1)}, bf16[896,256]{1,0:T(8,128)(2,1)S(1)}, u32[]{:S(2)}, u32[]{:S(2)}) collective-permute-start(bf16[896,256]{1,0:T(8,128)(2,1)S(1)} %get-tuple-element.50.refs_0_), channel_id=1, source_target_pairs={{0,1},{1,0},{2,3},{3,2},{4,5},{5,4},{6,7},{7,6},{8,9},{9,8},{10,11... | collective-permute-start | bytes 1376264 | tf_op jit(solution)/shard_map/ppermute | solution.py:553
  56.8 3.5 %collective-permute-start.13 = (bf16[4,4,2,64,128]{4,3,2,1,0:T(8,128)(2,1)S(1)}, bf16[4,4,2,64,128]{4,3,2,1,0:T(8,128)(2,1)S(1)}, u32[]{:S(2)}, u32[]{:S(2)}) collective-permute-start(bf16[4,4,2,64,128]{4,3,2,1,0:T(8,128)(2,1)S(1)} %pad_maximum_fusion.1.near), channel_id=1, source_target_pairs={{0,4},{4,0},{8,12},{12,8},{16,20},{20,16},{24,28},{28,24},{1,5},{5... | collective-permute-start | bytes 1572872 | tf_op jit(solution)/shard_map/ppermute | solution.py:553
  57.3 24.7 %collective-permute-start.12 = (bf16[128,1792]{1,0:T(8,128)(2,1)S(1)}, bf16[128,1792]{1,0:T(8,128)(2,1)S(1)}, u32[]{:S(2)}, u32[]{:S(2)}) collective-permute-start(bf16[128,1792]{1,0:T(8,128)(2,1)S(1)} %get-tuple-element.51.refs_0_), channel_id=1, source_target_pairs={{0,24},{4,28},{8,16},{12,20},{16,8},{20,12},{24,0},{28,4},{1,25},{... | collective-permute-start | bytes 1376264 | tf_op jit(solution)/shard_map/ppermute | solution.py:553
  59.5 22.5 %collective-permute-start.11 = (bf16[128,1792]{1,0:T(8,128)(2,1)S(1)}, bf16[128,1792]{1,0:T(8,128)(2,1)S(1)}, u32[]{:S(2)}, u32[]{:S(2)}) collective-permute-start(bf16[128,1792]{1,0:T(8,128)(2,1)S(1)} %get-tuple-element.51.refs_0_), channel_id=1, source_target_pairs={{0,16},{4,20},{8,24},{12,28},{16,0},{20,4},{24,8},{28,12},{1,17},{... | collective-permute-start | bytes 1376264 | tf_op jit(solution)/shard_map/ppermute | solution.py:553
  59.7 22.3 %collective-permute-start.10 = (bf16[128,1792]{1,0:T(8,128)(2,1)S(1)}, bf16[128,1792]{1,0:T(8,128)(2,1)S(1)}, u32[]{:S(2)}, u32[]{:S(2)}) collective-permute-start(bf16[128,1792]{1,0:T(8,128)(2,1)S(1)} %get-tuple-element.51.refs_0_), channel_id=1, source_target_pairs={{0,8},{4,12},{8,0},{12,4},{16,24},{20,28},{24,16},{28,20},{1,9},{5... | collective-permute-start | bytes 1376264 | tf_op jit(solution)/shard_map/ppermute | solution.py:553
  60.0 22.0 %collective-permute-start.14 = (bf16[896,256]{1,0:T(8,128)(2,1)S(1)}, bf16[896,256]{1,0:T(8,128)(2,1)S(1)}, u32[]{:S(2)}, u32[]{:S(2)}) collective-permute-start(bf16[896,256]{1,0:T(8,128)(2,1)S(1)} %get-tuple-element.50.refs_0_), channel_id=1, source_target_pairs={{0,2},{1,3},{2,0},{3,1},{4,6},{5,7},{6,4},{7,5},{8,10},{9,11},{10,... | collective-permute-start | bytes 1376264 | tf_op jit(solution)/shard_map/ppermute | solution.py:553
  82.2 5.9 %collective-permute-start.15 = (bf16[4,128,1792]{2,1,0:T(8,128)(2,1)S(1)}, bf16[4,128,1792]{2,1,0:T(8,128)(2,1)S(1)}, u32[]{:S(2)}, u32[]{:S(2)}) collective-permute-start(bf16[4,128,1792]{2,1,0:T(8,128)(2,1)S(1)} %pad_maximum_fusion), channel_id=1, source_target_pairs={{0,4},{4,0},{8,12},{12,8},{16,20},{20,16},{24,28},{28,24},{1,5},{5... | collective-permute-start | bytes 5505032 | tf_op jit(solution)/shard_map/ppermute | solution.py:553
  84.0 4.2 %copy-start.2 = (bf16[1024,2048]{1,0:T(8,128)(2,1)S(1)}, bf16[1024,2048]{1,0:T(8,128)(2,1)}, u32[]{:S(2)}) copy-start(bf16[1024,2048]{1,0:T(8,128)(2,1)} %copy-done.1) | copy-start | bytes 12582916
